TPU v7x, 256 devices: a whole 4x4x8 slice. The times are simulated.
256 devices in a mesh: occ: 8 (over x, y_hi), vir: 32 (over z, y_lo, core).
Axes of the slice: x: 4, y: 4 (y_hi: 2, y_lo: 2; y = y_hi * 2 + y_lo), z: 8, core: 2. Of those that a mesh axis runs over, the one named last changes fastest.
Arguments:
- amplitudes: bfloat16 [6144, 65536], P('occ', 'vir'), may hold values from -6 to 6
- integrals: bfloat16 [65536, 4096], P('vir', 'occ'), may hold values from -0.046875 to 0.046875
- other_terms: float32 [6144, 4096], P('occ', 'vir'), may hold values from -6 to 6
- occ_pairs: int32 [2, 6144], P(None, 'occ'), may hold values from 0 to 199
- vir_a: int32 [16], replicated, may hold values from 0 to 1999
- vir_b: int32 [256], replicated, may hold values from 0 to 1999
- eps_occ: float32 [200], replicated, may hold values from -3 to -0.3
- eps_vir: float32 [2000], replicated, may hold values from 0.2 to 3
Outputs:
- new_amplitudes: float32 [6144, 4096], P('occ', 'vir')
All inputs are finite; a program needn't handle non-finite values.
Results may differ from a plain program's by a relative error of at most 0.0003.
Values may be sent and summed in bfloat16 or wider, within the bound.
No kernel may reach another device: no remote copies, remote signals or barrier semaphores. Data moves between devices by JAX's collectives and lax.ppermute only.
A program may use at most 128 MiB of HBM per device.

v0:
```python
import jax
import jax.numpy as jnp
from jax import lax
from jax.sharding import PartitionSpec as P


def lookup(indices, table):
    positions = jnp.arange(table.shape[0], dtype=jnp.int32)
    return jnp.sum(jnp.where(indices[:, None] == positions[None, :], table[None, :], 0.0), axis=1)


def per_device(amplitudes, integrals, other_terms, occ_pairs, vir_a, vir_b, eps_occ, eps_vir):
    local_cols = other_terms.shape[1]
    partial_terms = jnp.dot(
        amplitudes,
        lax.all_gather(integrals, "occ", axis=1, tiled=True),
        preferred_element_type=jnp.float32,
    )
    ladder = lax.psum_scatter(partial_terms, "vir", scatter_dimension=1, tiled=True)
    first_col = lax.axis_index("vir") * local_cols
    global_col = first_col + jnp.arange(local_cols, dtype=jnp.int32)
    per_irrep = vir_b.shape[0]
    a_orbital = lookup(global_col // per_irrep, vir_a.astype(jnp.float32)).astype(jnp.int32)
    b_orbital = lookup(global_col % per_irrep, vir_b.astype(jnp.float32)).astype(jnp.int32)
    column_energy = lookup(a_orbital, eps_vir) + lookup(b_orbital, eps_vir)
    row_energy = lookup(occ_pairs[0], eps_occ) + lookup(occ_pairs[1], eps_occ)
    denominator = column_energy[None, :] - row_energy[:, None]
    return (other_terms + ladder) / denominator


def solution(mesh):
    in_specs = (
        P("occ", "vir"),
        P("vir", "occ"),
        P("occ", "vir"),
        P(None, "occ"),
        P(),
        P(),
        P(),
        P(),
    )
    out_specs = P("occ", "vir")
    return jax.shard_map(
        per_device, mesh=mesh, in_specs=in_specs, out_specs=out_specs, check_vma=False
    )
```

profile of v0, /device:TPU:32, one launch (start us, length us, event | category | flops | bytes accessed | tf_op | source)
XLA Modules:
  0.0 394.9 jit_solution(15334221738896634142)
XLA Ops:
  6.5 0.0 copy-start
  6.5 0.0 all-gather.2.cloned.1.call-start
  6.5 0.7 all-gather.2.cloned.1.call-update
  7.3 0.0 reduce-scatter.2.cloned.1.call-start
  7.3 216.3 %all-gather.2.cloned.1.call-done = bf16[2048,4096]{1,0:T(8,128)(2,1)} async-done(((bf16[2048,512]{1,0:T(8,128)(2,1)}), bf16[2048,4096]{1,0:T(8,128)(2,1)}) %all-gather.2.cloned.1.call-update) | async-done | bytes 16777232 | tf_op jit(solution)/shard_map/all_gather | solution.py:16
  223.7 0.0 copy-done
  223.7 19.3 %fusion = f32[768,4096]{1,0:T(8,128)} fusion(bf16[768,2048]{1,0:T(8,128)(2,1)S(1)} %copy-done, bf16[2048,4096]{1,0:T(8,128)(2,1)} %all-gather.2.cloned.1.call-done), kind=kOutput, calls=%fused_computation.21 | convolution fusion | flops 12884901888 | bytes 32505856 | tf_op jit(solution)/shard_map/dot_general | solution.py:14
  243.0 0.0 copy-start.3
  243.0 0.0 copy-start.2
  243.0 0.0 copy-start.1
  243.0 0.0 reduce-scatter.2.cloned.1.call-update
  243.0 1.3 convert_element_type.22
  244.3 0.9 select_reduce_fusion.4
  245.2 0.7 convert_element_type.20
  245.9 0.1 select_reduce_fusion.5
  246.0 0.0 copy-done.3
  246.0 0.9 select_reduce_fusion.2
  246.9 0.0 copy-done.2
  247.0 0.3 select_reduce_fusion
  247.3 138.9 %reduce-scatter.2.cloned.1.call-done = f32[768,128]{1,0:T(8,128)} async-done(((f32[768,4096]{1,0:T(8,128)}), f32[768,128]{1,0:T(8,128)}) %reduce-scatter.2.cloned.1.call-update) | async-done | bytes 393232 | tf_op jit(solution)/shard_map/reduce_scatter | solution.py:19
  386.2 0.0 copy-done.1
  386.2 1.9 subtract_divide_fusion
  (6 shorter events, 0.1 us)
Async XLA Ops:
  6.5 217.1 %copy-start = (bf16[768,2048]{1,0:T(8,128)(2,1)S(1)}, bf16[768,2048]{1,0:T(8,128)(2,1)}, u32[]{:S(2)}) copy-start(bf16[768,2048]{1,0:T(8,128)(2,1)} %param.8) | copy-start | bytes 9437188
  6.5 217.1 %all-gather.2.cloned.1.call-start = ((), (), s32[]{:S(2)}) async-start(), calls=%async_computation.1 | async-start | bytes 18874368 | tf_op jit(solution)/shard_map/all_gather | solution.py:16
  7.3 378.9 %reduce-scatter.2.cloned.1.call-start = ((), (), s32[]{:S(2)}) async-start(), calls=%async_computation.2 | async-start | bytes 12976128 | tf_op jit(solution)/shard_map/reduce_scatter | solution.py:19
  243.0 3.0 copy-start.3
  243.0 4.0 %copy-start.2 = (f32[2000]{0:T(1024)S(1)}, f32[2000]{0:T(1024)}, u32[]{:S(2)}) copy-start(f32[2000]{0:T(1024)} %param.15) | copy-start | bytes 24004
  243.0 143.2 %copy-start.1 = (f32[768,128]{1,0:T(8,128)S(1)}, f32[768,128]{1,0:T(8,128)}, u32[]{:S(2)}) copy-start(f32[768,128]{1,0:T(8,128)} %param.10) | copy-start | bytes 1179652
Sparse Core Ops, SparseCore 0:
  9.8 213.7 all-gather.1
  243.1 142.9 reduce-scatter.1
where the time goes:
time: 402 us; the launch traced here: 395 us
  waiting for transfers between devices  356 us (89%)
  matrix products  19.3 us (5%)
  between operations  13.5 us (3%)
  other arithmetic  6.13 us (2%)
    all_gather x1, waiting for transfers between devices, per_device(): lax.all_gather(integrals, 'occ', axis=1, tiled=True)  216 us
    reduce_scatter x1, waiting for transfers between devices, per_device(): lax.psum_scatter(partial_terms, 'vir', scatter_dimension=1, tiled=True)  139 us
    dot_general x1, matrix products, per_device(): jnp.dot(amplitudes, lax.all_gather(integrals, 'occ', axis=1, tiled=True),...  19.3 us
  transfers between devices with their start and end apart: 2, of which 2 were waited for; matrix products, arithmetic and copies ran while one was open for 1% of the time, Pallas kernels for 0%

commit v1 on v0

--- a/solution.py
+++ b/solution.py
@@ -2,6 +2,53 @@
 import jax.numpy as jnp
 from jax import lax
 from jax.sharding import PartitionSpec as P
+
+AXES = ("occ", "vir")
+NX, NYH, NZ, NYL, NC = 4, 2, 8, 2, 2
+SCALE_PART = 32.0
+SCALE_SUM = 4.0
+
+
+def device_id(x, yh, z, yl, c):
+    return ((x % NX) * NYH + yh % NYH) * (NZ * NYL * NC) + ((z % NZ) * NYL + yl % NYL) * NC + c % NC
+
+
+def everywhere():
+    return [
+        (x, yh, z, yl, c)
+        for x in range(NX)
+        for yh in range(NYH)
+        for z in range(NZ)
+        for yl in range(NYL)
+        for c in range(NC)
+    ]
+
+
+def moved(target):
+    return [(device_id(*spot), device_id(*target(*spot))) for spot in everywhere()]
+
+
+X_UP = moved(lambda x, yh, z, yl, c: (x + 1, yh, z, yl, c))
+X_DOWN = moved(lambda x, yh, z, yl, c: (x - 1, yh, z, yl, c))
+Y_FAR = moved(lambda x, yh, z, yl, c: (x, yh + 1, z, yl, c))
+CORE = moved(lambda x, yh, z, yl, c: (x, yh, z, yl, c + 1))
+HOME = moved(lambda x, yh, z, yl, c: (x, z % 2, z - z % 2 + yh, yl, c))
+HOME_NEXT = moved(lambda x, yh, z, yl, c: (x, z % 2, z - z % 2 + yh, yl + 1, c))
+Z_GROUPS = [
+    [device_id(x, yh, 2 * ((x + j // 2) % NX) + (yh + j % 2) % NYH, yl, c) for j in range(NZ)]
+    for x in range(NX)
+    for yh in range(NYH)
+    for yl in range(NYL)
+    for c in range(NC)
+]
+
+
+def send(block, route):
+    return lax.ppermute(block, AXES, route)
+
+
+def over_z(pieces):
+    return lax.all_to_all(pieces, AXES, 0, 0, axis_index_groups=Z_GROUPS, tiled=True)
 
 
 def lookup(indices, table):
@@ -9,16 +56,92 @@
     return jnp.sum(jnp.where(indices[:, None] == positions[None, :], table[None, :], 0.0), axis=1)
 
 
+def stripes(rows, cols):
+    out = jnp.dot(rows, cols, preferred_element_type=jnp.float32) * SCALE_PART
+    out = out.astype(jnp.float16)
+    units = rows.shape[0] // 256
+    return [out[256 * u : 256 * (u + 1)].reshape(NZ, 32, 256) for u in range(units)]
+
+
+def reduce_z(batch):
+    got = over_z(jnp.concatenate(batch, axis=1))
+    total = jnp.sum(got.astype(jnp.float32), axis=0) * (SCALE_SUM / SCALE_PART)
+    total = total.astype(jnp.float16)
+    return [total[32 * u : 32 * (u + 1)] for u in range(len(batch))]
+
+
 def per_device(amplitudes, integrals, other_terms, occ_pairs, vir_a, vir_b, eps_occ, eps_vir):
+    vir = lax.axis_index("vir")
+    core = vir % NC
+    y_low = (vir // NC) % NYL
+    barrier = lax.optimization_barrier
+
+    def columns(which, of_core):
+        return lax.dynamic_slice_in_dim(integrals, which * 256 + of_core * 128, 128, axis=1)
+
+    b = [
+        jnp.concatenate([columns(j, core), send(columns(j, 1 - core), CORE)], axis=0) for j in range(2)
+    ]
+    p1, m1, ay0 = send(b[0], X_UP), send(b[1], X_DOWN), send(amplitudes[:256], Y_FAR)
+    own = jnp.concatenate([amplitudes, send(amplitudes, CORE)], axis=1)
+    q0 = jnp.concatenate(b, axis=1)
+    s0 = reduce_z(stripes(own, q0))
+    p1, m1, ay0, a1 = barrier((p1, m1, ay0, amplitudes[256:512]))
+    p2, m2, ay1 = send(p1, X_UP), send(m1, X_DOWN), send(a1, Y_FAR)
+    far0 = jnp.concatenate([ay0, send(ay0, CORE)], axis=1)
+    q1 = jnp.concatenate([p1, m1], axis=1)
+    s1 = reduce_z(stripes(own, q1) + stripes(far0, q0) + stripes(far0, q1))
+    p2, m2, ay1, a2, b0, b1 = barrier((p2, m2, ay1, amplitudes[512:], b[0], b[1]))
+    p3, m3, ay2 = send(b1, X_UP), send(b0, X_DOWN), send(a2, Y_FAR)
+    far1 = jnp.concatenate([ay1, send(ay1, CORE)], axis=1)
+    q2 = jnp.concatenate([p2, m2], axis=1)
+    s2 = reduce_z(
+        stripes(own, q2) + stripes(far0, q2) + stripes(far1, q0) + stripes(far1, q1) + stripes(far1, q2)
+    )
+    far2 = jnp.concatenate([ay2, send(ay2, CORE)], axis=1)
+    q3 = jnp.concatenate([p3, m3], axis=1)
+    s3 = reduce_z(
+        stripes(own, q3)
+        + stripes(far0, q3)
+        + stripes(far1, q3)
+        + stripes(far2, q0)
+        + stripes(far2, q1)
+        + stripes(far2, q2)
+        + stripes(far2, q3)
+    )
+    held = {}
+    for u in range(3):
+        for q, s in enumerate((s0, s1, s2, s3)):
+            held[u, q] = s[u]
+    held[3, 0], held[3, 1] = s1[3], s1[4]
+    held[3, 2], held[4, 0], held[4, 1], held[4, 2] = s2[3], s2[4], s2[5], s2[6]
+    held[3, 3], held[4, 3] = s3[3], s3[4]
+    for q in range(4):
+        held[5, q] = s3[5 + q]
+    slots = []
+    for shift in range(4):
+        for far in range(2):
+            rows = []
+            for u in range(3):
+                at = [held[3 * far + u, q] for q in range(4)]
+                if shift == 0:
+                    rows.append(at[0])
+                elif shift == 1:
+                    rows.append(jnp.concatenate([at[3][:, 128:], at[1][:, 128:]], axis=1))
+                elif shift == 2:
+                    rows.append(at[2])
+                else:
+                    rows.append(jnp.concatenate([at[1][:, :128], at[3][:, :128]], axis=1))
+            slots.append(jnp.concatenate(rows, axis=0))
+    got = over_z(jnp.stack(slots))
+    got = got.reshape(NZ, 3, 32, 256).transpose(1, 0, 2, 3).reshape(768, 256)
+    mine = lax.dynamic_slice_in_dim(got, y_low * 128, 128, axis=1)
+    next_one = lax.dynamic_slice_in_dim(got, (1 - y_low) * 128, 128, axis=1)
+    mine, next_one = send(mine, HOME), send(next_one, HOME_NEXT)
+    ladder = (mine.astype(jnp.float32) + next_one.astype(jnp.float32)) * (1.0 / SCALE_SUM)
+
     local_cols = other_terms.shape[1]
-    partial_terms = jnp.dot(
-        amplitudes,
-        lax.all_gather(integrals, "occ", axis=1, tiled=True),
-        preferred_element_type=jnp.float32,
-    )
-    ladder = lax.psum_scatter(partial_terms, "vir", scatter_dimension=1, tiled=True)
-    first_col = lax.axis_index("vir") * local_cols
-    global_col = first_col + jnp.arange(local_cols, dtype=jnp.int32)
+    global_col = vir * local_cols + jnp.arange(local_cols, dtype=jnp.int32)
     per_irrep = vir_b.shape[0]
     a_orbital = lookup(global_col // per_irrep, vir_a.astype(jnp.float32)).astype(jnp.int32)
     b_orbital = lookup(global_col % per_irrep, vir_b.astype(jnp.float32)).astype(jnp.int32)

time: 402 us -> 234 us (0.58); the launches traced: 395 us -> 233 us
  waiting for transfers between devices: 356 us -> 116 us
  starting transfers between devices: 0.04 us -> 54.7 us
  local copies, waits for them, and re-layouts: 0.04 us -> 27.1 us
  between operations: 13.5 us -> 0.78 us
  matrix products: 19.3 us -> 25.1 us
    all_gather x1 -> x0, waiting for transfers between devices: 216 us -> none  [per_device(): lax.all_gather(integrals, 'occ', axis=1, tiled=True)]
    reduce_scatter x1 -> x0, waiting for transfers between devices: 139 us -> none  [per_device(): lax.psum_scatter(partial_terms, 'vir', scatter_dimension=1, tiled=True)]
    all_to_all x0 -> x5, waiting for transfers between devices: none -> 62.5 us  [over_z(): lax.all_to_all(pieces, AXES, 0, 0, axis_index_groups=Z_GROUPS, tiled=True)]
    ppermute x0 -> x17, waiting for transfers between devices: none -> 53 us  [send(): return lax.ppermute(block, AXES, route)]
    all_to_all x0 -> x5, starting transfers between devices: none -> 30.4 us  [over_z(): lax.all_to_all(pieces, AXES, 0, 0, axis_index_groups=Z_GROUPS, tiled=True)]
    ppermute x0 -> x17, starting transfers between devices: none -> 24.2 us  [send(): return lax.ppermute(block, AXES, route)]
    unnamed x8 -> x78, local copies, waits for them, and re-layouts: 0.02 us -> 16 us
    concatenate x0 -> x10, local copies, waits for them, and re-layouts: none -> 7.17 us  [the longest x1 2.39 us: per_device(): far2 = jnp.concatenate([ay2, send(ay2, CORE)], axis=1)]
  transfers between devices with their start and end apart: 2 -> 22, of which waited for: 2 -> 11; matrix products, arithmetic and copies ran while one was open for 1% -> 22% of each run, Pallas kernels for 0% -> 0%
where the time goes in v1:
time: 234 us; the launch traced here: 233 us
  waiting for transfers between devices  116 us (50%)
  starting transfers between devices  54.7 us (23%)
  local copies, waits for them, and re-layouts  27.1 us (12%)
  matrix products  25.1 us (11%)
  other arithmetic  9.88 us (4%)
    all_to_all x5, waiting for transfers between devices, over_z(): lax.all_to_all(pieces, AXES, 0, 0, axis_index_groups=Z_GROUPS, tiled=True)  62.5 us
    ppermute x17, waiting for transfers between devices, send(): return lax.ppermute(block, AXES, route)  53 us
    all_to_all x5, starting transfers between devices, over_z(): lax.all_to_all(pieces, AXES, 0, 0, axis_index_groups=Z_GROUPS, tiled=True)  30.4 us
    dot_general x16, matrix products, stripes(): out = jnp.dot(rows, cols, preferred_element_type=jnp.float32) * SCALE_PART  25.1 us
    ppermute x17, starting transfers between devices, send(): return lax.ppermute(block, AXES, route)  24.2 us
    unnamed x78, local copies, waits for them, and re-layouts  16 us
  transfers between devices with their start and end apart: 22, of which 11 were waited for; matrix products, arithmetic and copies ran while one was open for 22% of the time, Pallas kernels for 0%

profile of v1, /device:TPU:32, one launch (start us, length us, event | category | flops | bytes accessed | tf_op | source)
XLA Modules:
  0.0 233.1 jit_solution(12614025818138292884)
XLA Ops:
  4.0 3.2 %collective-permute-start.5 = (bf16[256,2048]{1,0:T(8,128)(2,1)S(1)}, bf16[256,2048]{1,0:T(8,128)(2,1)S(1)}, u32[]{:S(2)}, u32[]{:S(2)}) collective-permute-start(bf16[256,2048]{1,0:T(8,128)(2,1)S(1)} %get-tuple-element.32), channel_id=1, source_target_pairs={{0,32},{1,33},{2,34},{3,35},{4,36},{5,37},{6,38},{7,39},{8,40},{9,... | collective-permute-start | bytes 3145736 | tf_op jit(solution)/shard_map/ppermute | solution.py:47
  13.1 17.5 %collective-permute-done.5 = bf16[256,2048]{1,0:T(8,128)(2,1)S(1)} collective-permute-done((bf16[256,2048]{1,0:T(8,128)(2,1)S(1)}, bf16[256,2048]{1,0:T(8,128)(2,1)S(1)}, u32[]{:S(2)}, u32[]{:S(2)}) %collective-permute-start.5) | collective-permute-done | bytes 1048608 | tf_op jit(solution)/shard_map/ppermute | solution.py:47
  30.6 4.0 %collective-permute-done.3 = bf16[4096,128]{1,0:T(8,128)(2,1)S(1)} collective-permute-done((bf16[4096,128]{1,0:T(8,128)(2,1)}, bf16[4096,128]{1,0:T(8,128)(2,1)S(1)}, u32[]{:S(2)}, u32[]{:S(2)}) %collective-permute-start.3) | collective-permute-done | bytes 1048608 | tf_op jit(solution)/shard_map/ppermute | solution.py:47
  40.4 20.0 %collective-permute-done.7 = bf16[4096,128]{1,0:T(8,128)(2,1)S(1)} collective-permute-done((bf16[4096,128]{1,0:T(8,128)(2,1)S(1)}, bf16[4096,128]{1,0:T(8,128)(2,1)S(1)}, u32[]{:S(2)}, u32[]{:S(2)}) %collective-permute-start.7) | collective-permute-done | bytes 1048608 | tf_op jit(solution)/shard_map/ppermute | solution.py:47
  60.4 3.1 %collective-permute-done.9 = bf16[256,2048]{1,0:T(8,128)(2,1)} collective-permute-done((bf16[256,2048]{1,0:T(8,128)(2,1)S(1)}, bf16[256,2048]{1,0:T(8,128)(2,1)}, u32[]{:S(2)}, u32[]{:S(2)}) %collective-permute-start.9) | collective-permute-done | bytes 1048608 | tf_op jit(solution)/shard_map/ppermute | solution.py:47
  63.8 3.0 %collective-permute-start.12 = (bf16[4096,128]{1,0:T(8,128)(2,1)}, bf16[4096,128]{1,0:T(8,128)(2,1)}, u32[]{:S(2)}, u32[]{:S(2)}) collective-permute-start(bf16[4096,128]{1,0:T(8,128)(2,1)} %pad_maximum_fusion), channel_id=1, source_target_pairs={{0,192},{1,193},{2,194},{3,195},{4,196},{5,197},{6,198},{7,199},{8... | collective-permute-start | bytes 3145736 | tf_op jit(solution)/shard_map/ppermute | solution.py:47
  66.7 2.4 %constant_dynamic-update-slice_fusion.14 = bf16[256,4096]{1,0:T(8,128)(2,1)} fusion(bf16[256,2048]{1,0:T(8,128)(2,1)} %collective-permute-done.9), kind=kLoop, calls=%fused_computation.69 | loop fusion | bytes 2097152
  80.3 8.6 %all-to-all-start = ((f16[8,96,256]{2,1,0:T(8,128)(2,1)}), f16[8,96,256]{2,1,0:T(8,128)(2,1)S(1)}, u32[]{:S(2)}, u32[]{:S(2)}) async-start(f16[8,96,256]{2,1,0:T(8,128)(2,1)} %pad_maximum_fusion.2), calls=%async_computation | async-start | bytes 786432 | tf_op jit(solution)/shard_map/all_to_all | solution.py:51
  104.3 7.2 %all-to-all-start.1 = ((f16[8,160,256]{2,1,0:T(8,128)(2,1)}), f16[8,160,256]{2,1,0:T(8,128)(2,1)S(1)}, u32[]{:S(2)}, u32[]{:S(2)}) async-start(f16[8,160,256]{2,1,0:T(8,128)(2,1)} %copy-done.4), calls=%async_computation.1 | async-start | bytes 1310720 | tf_op jit(solution)/shard_map/all_to_all | solution.py:51
  111.6 2.9 %fusion.9 = f16[256,256]{1,0:T(8,128)(2,1)S(1)} fusion(bf16[256,4096]{1,0:T(8,128)(2,1)} %copy-done.6, bf16[4096,256]{1,0:T(8,128)(2,1)} %copy-done.11), kind=kOutput, calls=%fused_computation.29 | convolution fusion | flops 537001984 | bytes 4325376 | tf_op jit(solution)/shard_map/dot_general | solution.py:60
  114.6 2.7 %constant_dynamic-update-slice_fusion.25 = bf16[256,4096]{1,0:T(8,128)(2,1)} fusion(bf16[256,2048]{1,0:T(8,128)(2,1)} %collective-permute-done.13), kind=kLoop, calls=%fused_computation.80 | loop fusion | bytes 2097152
  117.3 2.4 %constant_dynamic-update-slice_fusion.24 = bf16[256,4096]{1,0:T(8,128)(2,1)} fusion(bf16[256,4096]{1,0:T(8,128)(2,1)} %constant_dynamic-update-slice_fusion.25, bf16[256,2048]{1,0:T(8,128)(2,1)} %collective-permute-done.14), kind=kLoop, calls=%fused_computation.79 | loop fusion | bytes 2097152 | tf_op jit(solution)/shard_map/concatenate | solution.py:101
  119.7 11.3 %all-to-all-done.1 = f16[8,160,256]{2,1,0:T(8,128)(2,1)S(1)} async-done(((f16[8,160,256]{2,1,0:T(8,128)(2,1)}), f16[8,160,256]{2,1,0:T(8,128)(2,1)S(1)}, u32[]{:S(2)}, u32[]{:S(2)}) %all-to-all-start.1) | async-done | bytes 655392 | tf_op jit(solution)/shard_map/all_to_all | solution.py:51
  131.0 4.9 %all-to-all-start.2 = ((f16[8,224,256]{2,1,0:T(8,128)(2,1)}), f16[8,224,256]{2,1,0:T(8,128)(2,1)S(1)}, u32[]{:S(2)}, u32[]{:S(2)}) async-start(f16[8,224,256]{2,1,0:T(8,128)(2,1)} %copy-done.3), calls=%async_computation.2 | async-start | bytes 1835008 | tf_op jit(solution)/shard_map/all_to_all | solution.py:51
  135.9 2.7 %fusion.12 = f16[256,256]{1,0:T(8,128)(2,1)S(1)} fusion(bf16[256,4096]{1,0:T(8,128)(2,1)} %constant_dynamic-update-slice_fusion.24, bf16[2048,128]{1,0:T(8,128)(2,1)} %copy-done.16, bf16[2048,128]{1,0:T(8,128)(2,1)S(1)} %get-tuple-element.37, bf16[2048,128]{1,0:T(8,128)(2,1)} %copy-done.18, bf16[2048,128]{1,0:T(8,128)(2,1)S(1)} %get-tuple-element.34), kind=kOutput, calls=%fused_computation.32 | convolution fusion | flops 545390592 | bytes 4325376 | tf_op jit(solution)/shard_map/dot_general | solution.py:60
  139.3 2.4 %fusion.13 = f16[256,256]{1,0:T(8,128)(2,1)S(1)} fusion(bf16[256,4096]{1,0:T(8,128)(2,1)} %constant_dynamic-update-slice_fusion.24, bf16[4096,256]{1,0:T(8,128)(2,1)S(1)} %copy-done.15), kind=kOutput, calls=%fused_computation.33 | convolution fusion | flops 537001984 | bytes 4325376 | tf_op jit(solution)/shard_map/dot_general | solution.py:60
  142.5 2.4 %fusion.14 = f16[256,256]{1,0:T(8,128)(2,1)S(1)} fusion(bf16[256,4096]{1,0:T(8,128)(2,1)} %constant_dynamic-update-slice_fusion.24, bf16[4096,256]{1,0:T(8,128)(2,1)S(1)} %copy-done.12), kind=kOutput, calls=%fused_computation.34 | convolution fusion | flops 537001984 | bytes 4325376 | tf_op jit(solution)/shard_map/dot_general | solution.py:60
  148.6 12.3 %all-to-all-done.2 = f16[8,224,256]{2,1,0:T(8,128)(2,1)S(1)} async-done(((f16[8,224,256]{2,1,0:T(8,128)(2,1)}), f16[8,224,256]{2,1,0:T(8,128)(2,1)S(1)}, u32[]{:S(2)}, u32[]{:S(2)}) %all-to-all-start.2) | async-done | bytes 917536 | tf_op jit(solution)/shard_map/all_to_all | solution.py:51
  160.9 4.9 %all-to-all-start.3 = ((f16[8,288,256]{2,1,0:T(8,128)(2,1)}), f16[8,288,256]{2,1,0:T(8,128)(2,1)S(1)}, u32[]{:S(2)}, u32[]{:S(2)}) async-start(f16[8,288,256]{2,1,0:T(8,128)(2,1)} %constant_dynamic-update-slice_fusion.26), calls=%async_computation.3 | async-start | bytes 2359296 | tf_op jit(solution)/shard_map/all_to_all | solution.py:51
  166.9 27.3 %all-to-all-done.3 = f16[8,288,256]{2,1,0:T(8,128)(2,1)S(1)} async-done(((f16[8,288,256]{2,1,0:T(8,128)(2,1)}), f16[8,288,256]{2,1,0:T(8,128)(2,1)S(1)}, u32[]{:S(2)}, u32[]{:S(2)}) %all-to-all-start.3) | async-done | bytes 1179680 | tf_op jit(solution)/shard_map/all_to_all | solution.py:51
  199.0 4.8 %all-to-all-start.4 = ((f16[8,96,256]{2,1,0:T(8,128)(2,1)}), f16[8,96,256]{2,1,0:T(8,128)(2,1)S(1)}, u32[]{:S(2)}, u32[]{:S(2)}) async-start(f16[8,96,256]{2,1,0:T(8,128)(2,1)} %constant_dynamic-update-slice_fusion.35), calls=%async_computation.4 | async-start | bytes 786432 | tf_op jit(solution)/shard_map/all_to_all | solution.py:51
  204.4 11.5 %all-to-all-done.4 = f16[8,96,256]{2,1,0:T(8,128)(2,1)S(1)} async-done(((f16[8,96,256]{2,1,0:T(8,128)(2,1)}), f16[8,96,256]{2,1,0:T(8,128)(2,1)S(1)}, u32[]{:S(2)}, u32[]{:S(2)}) %all-to-all-start.4) | async-done | bytes 393248 | tf_op jit(solution)/shard_map/all_to_all | solution.py:51
  216.1 6.1 %collective-permute-start.16 = (f16[768,128]{1,0:T(8,128)(2,1)S(1)}, f16[768,128]{1,0:T(8,128)(2,1)S(1)}, u32[]{:S(2)}, u32[]{:S(2)}) collective-permute-start(f16[768,128]{1,0:T(8,128)(2,1)S(1)} %get-tuple-element.39), channel_id=1, source_target_pairs={{0,2},{1,3},{2,0},{3,1},{4,34},{5,35},{6,32},{7,33},{8,10},{9,11},... | collective-permute-start | bytes 589832 | tf_op jit(solution)/shard_map/ppermute | solution.py:47
  226.3 5.8 %collective-permute-done.15 = f16[768,128]{1,0:T(8,128)(2,1)S(1)} collective-permute-done((f16[768,128]{1,0:T(8,128)(2,1)S(1)}, f16[768,128]{1,0:T(8,128)(2,1)S(1)}, u32[]{:S(2)}, u32[]{:S(2)}) %collective-permute-start.15) | collective-permute-done | bytes 196640 | tf_op jit(solution)/shard_map/ppermute | solution.py:47
  (167 shorter events, 58.8 us)
Async XLA Ops:
  1.9 8.0 %collective-permute-start.2 = (bf16[2048,128]{1,0:T(8,128)(2,1)S(1)}, bf16[2048,128]{1,0:T(8,128)(2,1)S(1)}, u32[]{:S(2)}, u32[]{:S(2)}) collective-permute-start(bf16[2048,128]{1,0:T(8,128)(2,1)S(1)} %get-tuple-element.36), channel_id=1, source_target_pairs={{0,1},{1,0},{2,3},{3,2},{4,5},{5,4},{6,7},{7,6},{8,9},{9,8},{10,11... | collective-permute-start | bytes 1572872 | tf_op jit(solution)/shard_map/ppermute | solution.py:47
  2.0 5.2 %collective-permute-start.1 = (bf16[2048,128]{1,0:T(8,128)(2,1)S(1)}, bf16[2048,128]{1,0:T(8,128)(2,1)S(1)}, u32[]{:S(2)}, u32[]{:S(2)}) collective-permute-start(bf16[2048,128]{1,0:T(8,128)(2,1)S(1)} %get-tuple-element.35), channel_id=1, source_target_pairs={{0,1},{1,0},{2,3},{3,2},{4,5},{5,4},{6,7},{7,6},{8,9},{9,8},{10,11... | collective-permute-start | bytes 1572872 | tf_op jit(solution)/shard_map/ppermute | solution.py:47
  4.0 26.6 %collective-permute-start.5 = (bf16[256,2048]{1,0:T(8,128)(2,1)S(1)}, bf16[256,2048]{1,0:T(8,128)(2,1)S(1)}, u32[]{:S(2)}, u32[]{:S(2)}) collective-permute-start(bf16[256,2048]{1,0:T(8,128)(2,1)S(1)} %get-tuple-element.32), channel_id=1, source_target_pairs={{0,32},{1,33},{2,34},{3,35},{4,36},{5,37},{6,38},{7,39},{8,40},{9,... | collective-permute-start | bytes 3145736 | tf_op jit(solution)/shard_map/ppermute | solution.py:47
  7.2 70.3 %copy-start.18 = (bf16[2048,128]{1,0:T(8,128)(2,1)}, bf16[2048,128]{1,0:T(8,128)(2,1)S(1)}, u32[]{:S(2)}) copy-start(bf16[2048,128]{1,0:T(8,128)(2,1)S(1)} %collective-permute-done.1) | copy-start | bytes 1572868
  8.3 26.2 %collective-permute-start.3 = (bf16[4096,128]{1,0:T(8,128)(2,1)}, bf16[4096,128]{1,0:T(8,128)(2,1)S(1)}, u32[]{:S(2)}, u32[]{:S(2)}) collective-permute-start(bf16[4096,128]{1,0:T(8,128)(2,1)} %pad_maximum_fusion), channel_id=1, source_target_pairs={{0,64},{1,65},{2,66},{3,67},{4,68},{5,69},{6,70},{7,71},{8,72},{9,... | collective-permute-start | bytes 3145736 | tf_op jit(solution)/shard_map/ppermute | solution.py:47
  9.8 67.7 %copy-start.16 = (bf16[2048,128]{1,0:T(8,128)(2,1)}, bf16[2048,128]{1,0:T(8,128)(2,1)S(1)}, u32[]{:S(2)}) copy-start(bf16[2048,128]{1,0:T(8,128)(2,1)S(1)} %collective-permute-done.2) | copy-start | bytes 1572868
  10.9 24.7 %collective-permute-start.4 = (bf16[4096,128]{1,0:T(8,128)(2,1)}, bf16[4096,128]{1,0:T(8,128)(2,1)S(1)}, u32[]{:S(2)}, u32[]{:S(2)}) collective-permute-start(bf16[4096,128]{1,0:T(8,128)(2,1)} %pad_maximum_fusion.1), channel_id=1, source_target_pairs={{0,192},{1,193},{2,194},{3,195},{4,196},{5,197},{6,198},{7,199},{8... | collective-permute-start | bytes 3145736 | tf_op jit(solution)/shard_map/ppermute | solution.py:47
  12.7 60.8 %collective-permute-start = (bf16[768,2048]{1,0:T(8,128)(2,1)S(1)}, bf16[768,2048]{1,0:T(8,128)(2,1)S(1)}, u32[]{:S(2)}, u32[]{:S(2)}) collective-permute-start(bf16[768,2048]{1,0:T(8,128)(2,1)S(1)} %copy-done), channel_id=1, source_target_pairs={{0,1},{1,0},{2,3},{3,2},{4,5},{5,4},{6,7},{7,6},{8,9},{9,8},{10,11... | collective-permute-start | bytes 9437192 | tf_op jit(solution)/shard_map/ppermute | solution.py:47
  35.6 24.8 %collective-permute-start.7 = (bf16[4096,128]{1,0:T(8,128)(2,1)S(1)}, bf16[4096,128]{1,0:T(8,128)(2,1)S(1)}, u32[]{:S(2)}, u32[]{:S(2)}) collective-permute-start(bf16[4096,128]{1,0:T(8,128)(2,1)S(1)} %collective-permute-done.3), channel_id=1, source_target_pairs={{0,64},{1,65},{2,66},{3,67},{4,68},{5,69},{6,70},{7,71},{8,72},{9,... | collective-permute-start | bytes 3145736 | tf_op jit(solution)/shard_map/ppermute | solution.py:47
  37.1 23.3 %collective-permute-start.8 = (bf16[4096,128]{1,0:T(8,128)(2,1)S(1)}, bf16[4096,128]{1,0:T(8,128)(2,1)S(1)}, u32[]{:S(2)}, u32[]{:S(2)}) collective-permute-start(bf16[4096,128]{1,0:T(8,128)(2,1)S(1)} %collective-permute-done.4), channel_id=1, source_target_pairs={{0,192},{1,193},{2,194},{3,195},{4,196},{5,197},{6,198},{7,199},{8... | collective-permute-start | bytes 3145736 | tf_op jit(solution)/shard_map/ppermute | solution.py:47
  38.9 24.6 %collective-permute-start.9 = (bf16[256,2048]{1,0:T(8,128)(2,1)S(1)}, bf16[256,2048]{1,0:T(8,128)(2,1)}, u32[]{:S(2)}, u32[]{:S(2)}) collective-permute-start(bf16[256,2048]{1,0:T(8,128)(2,1)S(1)} %get-tuple-element.18), channel_id=1, source_target_pairs={{0,32},{1,33},{2,34},{3,35},{4,36},{5,37},{6,38},{7,39},{8,40},{9,... | collective-permute-start | bytes 3145736 | tf_op jit(solution)/shard_map/ppermute | solution.py:47
  39.9 29.2 %collective-permute-start.6 = (bf16[256,2048]{1,0:T(8,128)(2,1)S(1)}, bf16[256,2048]{1,0:T(8,128)(2,1)S(1)}, u32[]{:S(2)}, u32[]{:S(2)}) collective-permute-start(bf16[256,2048]{1,0:T(8,128)(2,1)S(1)} %collective-permute-done.5), channel_id=1, source_target_pairs={{0,1},{1,0},{2,3},{3,2},{4,5},{5,4},{6,7},{7,6},{8,9},{9,8},{10,11... | collective-permute-start | bytes 3145736 | tf_op jit(solution)/shard_map/ppermute | solution.py:47
  63.5 25.8 %collective-permute-start.11 = (bf16[4096,128]{1,0:T(8,128)(2,1)}, bf16[4096,128]{1,0:T(8,128)(2,1)}, u32[]{:S(2)}, u32[]{:S(2)}) collective-permute-start(bf16[4096,128]{1,0:T(8,128)(2,1)} %pad_maximum_fusion.1), channel_id=1, source_target_pairs={{0,64},{1,65},{2,66},{3,67},{4,68},{5,69},{6,70},{7,71},{8,72},{9,... | collective-permute-start | bytes 3145736 | tf_op jit(solution)/shard_map/ppermute | solution.py:47
  63.8 27.3 %collective-permute-start.12 = (bf16[4096,128]{1,0:T(8,128)(2,1)}, bf16[4096,128]{1,0:T(8,128)(2,1)}, u32[]{:S(2)}, u32[]{:S(2)}) collective-permute-start(bf16[4096,128]{1,0:T(8,128)(2,1)} %pad_maximum_fusion), channel_id=1, source_target_pairs={{0,192},{1,193},{2,194},{3,195},{4,196},{5,197},{6,198},{7,199},{8... | collective-permute-start | bytes 3145736 | tf_op jit(solution)/shard_map/ppermute | solution.py:47
  66.7 30.2 %collective-permute-start.10 = (bf16[256,2048]{1,0:T(8,128)(2,1)}, bf16[256,2048]{1,0:T(8,128)(2,1)}, u32[]{:S(2)}, u32[]{:S(2)}) collective-permute-start(bf16[256,2048]{1,0:T(8,128)(2,1)} %collective-permute-done.9), channel_id=1, source_target_pairs={{0,1},{1,0},{2,3},{3,2},{4,5},{5,4},{6,7},{7,6},{8,9},{9,8},{10,11... | collective-permute-start | bytes 3145736 | tf_op jit(solution)/shard_map/ppermute | solution.py:47
  69.1 33.1 %collective-permute-start.13 = (bf16[256,2048]{1,0:T(8,128)(2,1)}, bf16[256,2048]{1,0:T(8,128)(2,1)}, u32[]{:S(2)}, u32[]{:S(2)}) collective-permute-start(bf16[256,2048]{1,0:T(8,128)(2,1)} %get-tuple-element.24), channel_id=1, source_target_pairs={{0,32},{1,33},{2,34},{3,35},{4,36},{5,37},{6,38},{7,39},{8,40},{9,... | collective-permute-start | bytes 3145736 | tf_op jit(solution)/shard_map/ppermute | solution.py:47
  80.3 24.0 %all-to-all-start = ((f16[8,96,256]{2,1,0:T(8,128)(2,1)}), f16[8,96,256]{2,1,0:T(8,128)(2,1)S(1)}, u32[]{:S(2)}, u32[]{:S(2)}) async-start(f16[8,96,256]{2,1,0:T(8,128)(2,1)} %pad_maximum_fusion.2), calls=%async_computation | async-start | bytes 786432 | tf_op jit(solution)/shard_map/all_to_all | solution.py:51
  102.2 15.1 %collective-permute-start.14 = (bf16[256,2048]{1,0:T(8,128)(2,1)}, bf16[256,2048]{1,0:T(8,128)(2,1)}, u32[]{:S(2)}, u32[]{:S(2)}) collective-permute-start(bf16[256,2048]{1,0:T(8,128)(2,1)} %collective-permute-done.13), channel_id=1, source_target_pairs={{0,1},{1,0},{2,3},{3,2},{4,5},{5,4},{6,7},{7,6},{8,9},{9,8},{10,11... | collective-permute-start | bytes 3145736 | tf_op jit(solution)/shard_map/ppermute | solution.py:47
  104.3 26.7 %all-to-all-start.1 = ((f16[8,160,256]{2,1,0:T(8,128)(2,1)}), f16[8,160,256]{2,1,0:T(8,128)(2,1)S(1)}, u32[]{:S(2)}, u32[]{:S(2)}) async-start(f16[8,160,256]{2,1,0:T(8,128)(2,1)} %copy-done.4), calls=%async_computation.1 | async-start | bytes 1310720 | tf_op jit(solution)/shard_map/all_to_all | solution.py:51
  131.0 29.9 %all-to-all-start.2 = ((f16[8,224,256]{2,1,0:T(8,128)(2,1)}), f16[8,224,256]{2,1,0:T(8,128)(2,1)S(1)}, u32[]{:S(2)}, u32[]{:S(2)}) async-start(f16[8,224,256]{2,1,0:T(8,128)(2,1)} %copy-done.3), calls=%async_computation.2 | async-start | bytes 1835008 | tf_op jit(solution)/shard_map/all_to_all | solution.py:51
  160.9 33.3 %all-to-all-start.3 = ((f16[8,288,256]{2,1,0:T(8,128)(2,1)}), f16[8,288,256]{2,1,0:T(8,128)(2,1)S(1)}, u32[]{:S(2)}, u32[]{:S(2)}) async-start(f16[8,288,256]{2,1,0:T(8,128)(2,1)} %constant_dynamic-update-slice_fusion.26), calls=%async_computation.3 | async-start | bytes 2359296 | tf_op jit(solution)/shard_map/all_to_all | solution.py:51
  199.0 16.9 %all-to-all-start.4 = ((f16[8,96,256]{2,1,0:T(8,128)(2,1)}), f16[8,96,256]{2,1,0:T(8,128)(2,1)S(1)}, u32[]{:S(2)}, u32[]{:S(2)}) async-start(f16[8,96,256]{2,1,0:T(8,128)(2,1)} %constant_dynamic-update-slice_fusion.35), calls=%async_computation.4 | async-start | bytes 786432 | tf_op jit(solution)/shard_map/all_to_all | solution.py:51
  216.1 10.3 %collective-permute-start.16 = (f16[768,128]{1,0:T(8,128)(2,1)S(1)}, f16[768,128]{1,0:T(8,128)(2,1)S(1)}, u32[]{:S(2)}, u32[]{:S(2)}) collective-permute-start(f16[768,128]{1,0:T(8,128)(2,1)S(1)} %get-tuple-element.39), channel_id=1, source_target_pairs={{0,2},{1,3},{2,0},{3,1},{4,34},{5,35},{6,32},{7,33},{8,10},{9,11},... | collective-permute-start | bytes 589832 | tf_op jit(solution)/shard_map/ppermute | solution.py:47
  222.2 10.0 %collective-permute-start.15 = (f16[768,128]{1,0:T(8,128)(2,1)S(1)}, f16[768,128]{1,0:T(8,128)(2,1)S(1)}, u32[]{:S(2)}, u32[]{:S(2)}) collective-permute-start(f16[768,128]{1,0:T(8,128)(2,1)S(1)} %get-tuple-element.38), channel_id=1, source_target_pairs={{0,0},{1,1},{2,2},{3,3},{4,32},{5,33},{6,34},{7,35},{8,8},{9,9},{1... | collective-permute-start | bytes 589832 | tf_op jit(solution)/shard_map/ppermute | solution.py:47
  (24 other events, 305.6 us)

commit v2 on v0

--- a/solution.py
+++ b/solution.py
@@ -1,7 +1,57 @@
 import jax
 import jax.numpy as jnp
 from jax import lax
+from jax.experimental import pallas as pl
+from jax.experimental.pallas import tpu as pltpu
 from jax.sharding import PartitionSpec as P
+
+AXES = ("occ", "vir")
+NX, NYH, NZ, NYL, NC = 4, 2, 8, 2, 2
+SCALE_CHIP = 32.0
+SCALE_PAIR = 16.0
+
+
+def device_id(x, yh, z, yl, c):
+    return ((x % NX) * NYH + yh % NYH) * (NZ * NYL * NC) + ((z % NZ) * NYL + yl % NYL) * NC + c % NC
+
+
+def everywhere():
+    return [
+        (x, yh, z, yl, c)
+        for x in range(NX)
+        for yh in range(NYH)
+        for z in range(NZ)
+        for yl in range(NYL)
+        for c in range(NC)
+    ]
+
+
+def moved(target):
+    return [(device_id(*spot), device_id(*target(*spot))) for spot in everywhere()]
+
+
+X_UP = moved(lambda x, yh, z, yl, c: (x + 1, yh, z, yl, c))
+X_DOWN = moved(lambda x, yh, z, yl, c: (x - 1, yh, z, yl, c))
+Y_FAR = moved(lambda x, yh, z, yl, c: (x, yh + 1, z, yl, c))
+CORE = moved(lambda x, yh, z, yl, c: (x, yh, z, yl, c + 1))
+Y_NEAR = moved(lambda x, yh, z, yl, c: (x, yh, z, yl + 1, c))
+
+
+Z_GROUPS = [
+    [device_id(x, yh, z, yl, c) for z in range(NZ)]
+    for x in range(NX)
+    for yh in range(NYH)
+    for yl in range(NYL)
+    for c in range(NC)
+]
+
+
+def send(block, route):
+    return lax.ppermute(block, AXES, route)
+
+
+def over_z(pieces):
+    return lax.all_to_all(pieces, AXES, 0, 0, axis_index_groups=Z_GROUPS, tiled=True)
 
 
 def lookup(indices, table):
@@ -9,16 +59,142 @@
     return jnp.sum(jnp.where(indices[:, None] == positions[None, :], table[None, :], 0.0), axis=1)
 
 
+def products(rows, cols, plan):
+    where = [(i, u) for i, pair in enumerate(rows) for u in range(pair[0].shape[0] // 256)]
+    row_arrays = [half for pair in rows for half in pair]
+    col_arrays = [chunk for pair in cols for chunk in pair]
+    n_rows, depth = len(row_arrays), rows[0][0].shape[1]
+
+    def kernel(*refs):
+        row_refs, col_refs, out_ref = refs[:n_rows], refs[n_rows:-1], refs[-1]
+        for at, (unit, pair) in enumerate(plan):
+            array, block = where[unit]
+            total = None
+            for half in range(2):
+                joined = jnp.concatenate(
+                    [col_refs[2 * pair + j][pl.ds(half * depth, depth), :] for j in range(2)], axis=1
+                )
+                left = row_refs[2 * array + half][pl.ds(256 * block, 256), :]
+                term = jnp.dot(left, joined, preferred_element_type=jnp.float32)
+                total = term if total is None else total + term
+            out_ref[:, pl.ds(32 * at, 32), :] = total.reshape(NZ, 32, 256)
+
+    in_vmem = pl.BlockSpec(memory_space=pltpu.VMEM)
+    return pl.pallas_call(
+        kernel,
+        out_shape=jax.ShapeDtypeStruct((NZ, 32 * len(plan), 256), jnp.float32),
+        in_specs=[in_vmem] * (n_rows + len(col_arrays)),
+        out_specs=in_vmem,
+        compiler_params=pltpu.CompilerParams(vmem_limit_bytes=16 * 1024 * 1024),
+        cost_estimate=pl.CostEstimate(flops=1, bytes_accessed=1, transcendentals=0),
+    )(*[pltpu.with_memory_space_constraint(array, pltpu.VMEM) for array in row_arrays + col_arrays])
+
+
+def half_precision(block, scale):
+    return (block * scale).astype(jnp.float16)
+
+
+def reduce_z(batch, scale):
+    return jnp.sum(over_z(batch).astype(jnp.float32), axis=0) * (1.0 / scale)
+
+
+def slots_of(places, early, late, early_far, late_far):
+    def kernel(places_ref, early_ref, late_ref, early_far_ref, late_far_ref, out_ref):
+        for q in range(4):
+            own, at = (early_ref, 96 * q) if q < 3 else (late_ref, 0)
+            out_ref[places_ref[2 * q]] = own[pl.ds(at, 96), :]
+            place = places_ref[2 * q + 1]
+            for unit in range(3):
+                ref, order = (
+                    (early_far_ref, EARLY_FAR) if (3 + unit, q) in EARLY_FAR else (late_far_ref, LATE_FAR)
+                )
+                at = 32 * order.index((3 + unit, q))
+                out_ref[place, pl.ds(32 * unit, 32), :] = ref[pl.ds(at, 32), :]
+
+    in_vmem = pl.BlockSpec(memory_space=pltpu.VMEM)
+    return pl.pallas_call(
+        kernel,
+        out_shape=jax.ShapeDtypeStruct((NZ, 96, 128), jnp.float32),
+        in_specs=[pl.BlockSpec(memory_space=pltpu.SMEM)] + [in_vmem] * 4,
+        out_specs=in_vmem,
+    )(places, early, late, early_far, late_far)
+
+
+PLAN = [
+    [(u, 0) for u in range(3)],
+    [(u, 1) for u in range(3)] + [(3, 0), (3, 1)],
+    [(u, 2) for u in range(4)] + [(4, q) for q in range(3)],
+    [(u, 3) for u in range(5)],
+    [(5, q) for q in range(4)],
+]
+EARLY_FAR = PLAN[1][3:] + PLAN[2][3:]
+LATE_FAR = PLAN[3][3:] + PLAN[4]
+
+
 def per_device(amplitudes, integrals, other_terms, occ_pairs, vir_a, vir_b, eps_occ, eps_vir):
+    vir = lax.axis_index("vir")
+    core = vir % NC
+    y_low = (vir // NC) % NYL
+    barrier = lax.optimization_barrier
+
+    def columns(which, of_core):
+        return lax.dynamic_slice_in_dim(integrals, which * 256 + of_core * 128, 128, axis=1)
+
+    x, y_high = lax.axis_index("occ") // NYH, lax.axis_index("occ") % NYH
+    shifts = [0, 3 - 2 * y_low, 2, 1 + 2 * y_low]
+    places = jnp.stack(
+        [2 * ((x + shift) % NX) + (y_high + far) % NYH for shift in shifts for far in range(2)]
+    ).astype(jnp.int32)
+
+    def mine(block):
+        return lax.dynamic_slice_in_dim(block, y_low * 128, 128, axis=block.ndim - 1)
+
+    def neighbours(block):
+        return lax.dynamic_slice_in_dim(block, (1 - y_low) * 128, 128, axis=block.ndim - 1)
+
+    b = tuple(
+        jnp.concatenate([columns(j, core), send(columns(j, 1 - core), CORE)], axis=0) for j in range(2)
+    )
+    p1, m1, ay0 = send(b[0], X_UP), send(b[1], X_DOWN), send(amplitudes[:256], Y_FAR)
+    rows = [(amplitudes, send(amplitudes, CORE))]
+    cols = [b]
+    in0 = half_precision(products(rows, cols, PLAN[0]), SCALE_CHIP)
+    s0 = reduce_z(in0, SCALE_CHIP)
+    p1, m1, ay0, later, in0 = barrier((p1, m1, ay0, amplitudes, in0))
+    p2, m2, ay1 = send(p1, X_UP), send(m1, X_DOWN), send(later[256:512], Y_FAR)
+    far = send(ay0, CORE)
+    rows, cols = rows + [(ay0, far)], cols + [(p1, m1)]
+    new, s0 = barrier((products(rows, cols, PLAN[1]), s0))
+    in1 = half_precision(new, SCALE_CHIP)
+    s1 = reduce_z(in1, SCALE_CHIP)
+    p2, m2, ay1, later, b0, b1, in1 = barrier((p2, m2, ay1, amplitudes, b[0], b[1], in1))
+    p3, m3, ay2 = send(b1, X_UP), send(b0, X_DOWN), send(later[512:], Y_FAR)
+    far = send(ay1, CORE)
+    rows, cols = rows + [(ay1, far)], cols + [(p2, m2)]
+    new, s1 = barrier((products(rows, cols, PLAN[2]), s1))
+    in2 = half_precision(new, SCALE_CHIP)
+    s2 = reduce_z(in2, SCALE_CHIP)
+    p3, m3, ay2, in2 = barrier((p3, m3, ay2, in2))
+    cols = cols + [(m3, p3)]
+    last = [
+        products(rows, cols[3:], [(u, 0) for u, _ in PLAN[3]]),
+        products([(ay2, send(ay2, CORE))], cols, [(0, q) for _, q in PLAN[4]]),
+    ]
+    last[1], s2 = barrier((last[1], s2))
+    met = [send(half_precision(neighbours(part), SCALE_CHIP), Y_NEAR) for part in last]
+    pair = [
+        half_precision(mine(part) + got.astype(jnp.float32) * (1.0 / SCALE_CHIP), SCALE_PAIR)
+        for part, got in zip(last, met)
+    ]
+    late = reduce_z(jnp.concatenate(pair, axis=1), SCALE_PAIR)
+    early = jnp.concatenate([s0, s1[:96], s2[:96], s1[96:], s2[96:]], axis=0)
+    early = mine(early) + send(neighbours(early), Y_NEAR)
+    early_far, late_far = send(early[288:], Y_FAR), send(late[96:], Y_FAR)
+    ladder = over_z(slots_of(places, early, late, early_far, late_far))
+    ladder = ladder.reshape(NZ, 3, 32, 128).transpose(1, 0, 2, 3).reshape(768, 128)
+
     local_cols = other_terms.shape[1]
-    partial_terms = jnp.dot(
-        amplitudes,
-        lax.all_gather(integrals, "occ", axis=1, tiled=True),
-        preferred_element_type=jnp.float32,
-    )
-    ladder = lax.psum_scatter(partial_terms, "vir", scatter_dimension=1, tiled=True)
-    first_col = lax.axis_index("vir") * local_cols
-    global_col = first_col + jnp.arange(local_cols, dtype=jnp.int32)
+    global_col = vir * local_cols + jnp.arange(local_cols, dtype=jnp.int32)
     per_irrep = vir_b.shape[0]
     a_orbital = lookup(global_col // per_irrep, vir_a.astype(jnp.float32)).astype(jnp.int32)
     b_orbital = lookup(global_col % per_irrep, vir_b.astype(jnp.float32)).astype(jnp.int32)

time: 402 us -> 182 us (0.45); the launches traced: 395 us -> 181 us
  waiting for transfers between devices: 356 us -> 57.5 us
  starting transfers between devices: 0.04 us -> 62.9 us
  Pallas kernels: 0 us -> 33.8 us
  matrix products: 19.3 us -> 0 us
  between operations: 13.5 us -> 0.43 us
  local copies, waits for them, and re-layouts: 0.04 us -> 11.9 us
  other arithmetic: 6.13 us -> 14.2 us
    all_gather x1 -> x0, waiting for transfers between devices: 216 us -> none  [per_device(): lax.all_gather(integrals, 'occ', axis=1, tiled=True)]
    reduce_scatter x1 -> x0, waiting for transfers between devices: 139 us -> none  [per_device(): lax.psum_scatter(partial_terms, 'vir', scatter_dimension=1, tiled=True)]
    all_to_all x0 -> x5, starting transfers between devices: none -> 37.3 us  [over_z(): lax.all_to_all(pieces, AXES, 0, 0, axis_index_groups=Z_GROUPS, tiled=True)]
    pallas_call x0 -> x6, Pallas kernels: none -> 33.8 us  [the longest x5 31.9 us: products(): pl.pallas_call(kernel, out_shape=jax.ShapeDtypeStruct((NZ, 32 * len(plan)...]
    ppermute x0 -> x20, waiting for transfers between devices: none -> 33.4 us  [send(): return lax.ppermute(block, AXES, route)]
    ppermute x0 -> x20, starting transfers between devices: none -> 25.6 us  [send(): return lax.ppermute(block, AXES, route)]
    all_to_all x0 -> x5, waiting for transfers between devices: none -> 24.1 us  [over_z(): lax.all_to_all(pieces, AXES, 0, 0, axis_index_groups=Z_GROUPS, tiled=True)]
    dot_general x1 -> x0, matrix products: 19.3 us -> none  [per_device(): jnp.dot(amplitudes, lax.all_gather(integrals, 'occ', axis=1, tiled=True),...]
  transfers between devices with their start and end apart: 2 -> 25, of which waited for: 2 -> 12; matrix products, arithmetic and copies ran while one was open for 1% -> 10% of each run, Pallas kernels for 0% -> 18%
where the time goes in v2:
time: 182 us; the launch traced here: 181 us
  starting transfers between devices  62.9 us (35%)
  waiting for transfers between devices  57.5 us (32%)
  Pallas kernels  33.8 us (19%)
  other arithmetic  14.2 us (8%)
  local copies, waits for them, and re-layouts  11.9 us (7%)
    all_to_all x5, starting transfers between devices, over_z(): lax.all_to_all(pieces, AXES, 0, 0, axis_index_groups=Z_GROUPS, tiled=True)  37.3 us
    ppermute x20, waiting for transfers between devices, send(): return lax.ppermute(block, AXES, route)  33.4 us
    pallas_call x5, Pallas kernels, products(): pl.pallas_call(kernel, out_shape=jax.ShapeDtypeStruct((NZ, 32 * len(plan)...  31.9 us
    ppermute x20, starting transfers between devices, send(): return lax.ppermute(block, AXES, route)  25.6 us
    all_to_all x5, waiting for transfers between devices, over_z(): lax.all_to_all(pieces, AXES, 0, 0, axis_index_groups=Z_GROUPS, tiled=True)  24.1 us
    convert_element_type x7, other arithmetic, half_precision(): return (block * scale).astype(jnp.float16)  6.52 us
    unnamed x40, local copies, waits for them, and re-layouts  6.08 us
  transfers between devices with their start and end apart: 25, of which 12 were waited for; matrix products, arithmetic and copies ran while one was open for 10% of the time, Pallas kernels for 18%

profile of v2, /device:TPU:32, one launch (start us, length us, event | category | flops | bytes accessed | tf_op | source)
XLA Modules:
  0.0 180.7 jit_solution(15865320865456245107)
XLA Ops:
  3.7 3.2 %collective-permute-start.5 = (bf16[256,2048]{1,0:T(8,128)(2,1)}, bf16[256,2048]{1,0:T(8,128)(2,1)}, u32[]{:S(2)}, u32[]{:S(2)}) collective-permute-start(bf16[256,2048]{1,0:T(8,128)(2,1)} %slice.33), channel_id=1, source_target_pairs={{0,32},{1,33},{2,34},{3,35},{4,36},{5,37},{6,38},{7,39},{8,40},{9,... | collective-permute-start | bytes 3145736 | tf_op jit(solution)/shard_map/ppermute | solution.py:50
  7.9 2.8 %collective-permute-start.4 = (bf16[4096,128]{1,0:T(8,128)(2,1)}, bf16[4096,128]{1,0:T(8,128)(2,1)}, u32[]{:S(2)}, u32[]{:S(2)}) collective-permute-start(bf16[4096,128]{1,0:T(8,128)(2,1)} %pad_maximum_fusion.1.refs_3_.refs_5_.refs_7_), channel_id=1, source_target_pairs={{0,192},{1,193},{2,194},{3,195},{4,196},{5,197},{6,198},{7,199},{8... | collective-permute-start | bytes 3145736 | tf_op jit(solution)/shard_map/ppermute | solution.py:50
  11.8 4.3 %shard_map.82 = f32[8,96,256]{2,1,0:T(8,128)S(1)} custom-call(bf16[768,2048]{1,0:T(8,128)(2,1)S(1)} %copy-done, bf16[768,2048]{1,0:T(8,128)(2,1)} %collective-permute-done.refs_1_, bf16[4096,128]{1,0:T(8,128)(2,1)} %pad_maximum_fusion.refs_2_.refs_4_.refs_6_, bf16[4096,128]{1,0:T(8,128)(2,1)} %pad_maximum_fusion.1.refs_3_.refs_5_.refs_7_), custom_call_target="tpu_custom_call" | custom-call | flops 1 | bytes 1 | tf_op jit(solution)/shard_map/pallas_call | solution.py:83
  16.9 8.6 %all-to-all-start = ((f16[8,96,256]{2,1,0:T(8,128)(2,1)}), f16[8,96,256]{2,1,0:T(8,128)(2,1)S(1)}, u32[]{:S(2)}, u32[]{:S(2)}) async-start(f16[8,96,256]{2,1,0:T(8,128)(2,1)} %multiply_convert_fusion.2), calls=%async_computation | async-start | bytes 786432 | tf_op jit(solution)/shard_map/all_to_all | solution.py:54
  25.5 5.6 %collective-permute-done.5.refs_2_ = bf16[256,2048]{1,0:T(8,128)(2,1)} collective-permute-done((bf16[256,2048]{1,0:T(8,128)(2,1)}, bf16[256,2048]{1,0:T(8,128)(2,1)}, u32[]{:S(2)}, u32[]{:S(2)}) %collective-permute-start.5) | collective-permute-done | bytes 1048608 | tf_op jit(solution)/shard_map/ppermute | solution.py:50
  31.1 2.8 %collective-permute-done.4.refs_7_.refs_9_.refs_5_ = bf16[4096,128]{1,0:T(8,128)(2,1)} collective-permute-done((bf16[4096,128]{1,0:T(8,128)(2,1)}, bf16[4096,128]{1,0:T(8,128)(2,1)}, u32[]{:S(2)}, u32[]{:S(2)}) %collective-permute-start.4) | collective-permute-done | bytes 1048608 | tf_op jit(solution)/shard_map/ppermute | solution.py:50
  33.8 4.5 %collective-permute-done.2.refs_6_.refs_8_.refs_4_ = bf16[4096,128]{1,0:T(8,128)(2,1)} collective-permute-done((bf16[4096,128]{1,0:T(8,128)(2,1)}, bf16[4096,128]{1,0:T(8,128)(2,1)}, u32[]{:S(2)}, u32[]{:S(2)}) %collective-permute-start.2) | collective-permute-done | bytes 1048608 | tf_op jit(solution)/shard_map/ppermute | solution.py:50
  42.0 3.2 %collective-permute-start.8 = (bf16[4096,128]{1,0:T(8,128)(2,1)}, bf16[4096,128]{1,0:T(8,128)(2,1)}, u32[]{:S(2)}, u32[]{:S(2)}) collective-permute-start(bf16[4096,128]{1,0:T(8,128)(2,1)} %collective-permute-done.4.refs_7_.refs_9_.refs_5_), channel_id=1, source_target_pairs={{0,192},{1,193},{2,194},{3,195},{4,196},{5,197},{6,198},{7,199},{8... | collective-permute-start | bytes 3145736 | tf_op jit(solution)/shard_map/ppermute | solution.py:50
  45.4 6.5 %shard_map.83 = f32[8,160,256]{2,1,0:T(8,128)S(1)} custom-call(bf16[768,2048]{1,0:T(8,128)(2,1)S(1)} %copy-done, bf16[768,2048]{1,0:T(8,128)(2,1)} %collective-permute-done.refs_1_, bf16[256,2048]{1,0:T(8,128)(2,1)} %collective-permute-done.5.refs_2_, bf16[256,2048]{1,0:T(8,128)(2,1)} %collective-permute-done.6.refs_3_, ...), custom_call_target="tpu_custom_call" | custom-call | flops 1 | bytes 1 | tf_op jit(solution)/shard_map/pallas_call | solution.py:83
  52.9 8.6 %all-to-all-start.1 = ((f16[8,160,256]{2,1,0:T(8,128)(2,1)}), f16[8,160,256]{2,1,0:T(8,128)(2,1)}, u32[]{:S(2)}, u32[]{:S(2)}) async-start(f16[8,160,256]{2,1,0:T(8,128)(2,1)} %multiply_convert_fusion.1), calls=%async_computation.1 | async-start | bytes 1310720 | tf_op jit(solution)/shard_map/all_to_all | solution.py:54
  61.5 5.3 %collective-permute-done.9.refs_4_ = bf16[256,2048]{1,0:T(8,128)(2,1)} collective-permute-done((bf16[256,2048]{1,0:T(8,128)(2,1)}, bf16[256,2048]{1,0:T(8,128)(2,1)}, u32[]{:S(2)}, u32[]{:S(2)}) %collective-permute-start.9) | collective-permute-done | bytes 1048608 | tf_op jit(solution)/shard_map/ppermute | solution.py:50
  70.8 3.2 %collective-permute-start.12 = (bf16[4096,128]{1,0:T(8,128)(2,1)}, bf16[4096,128]{1,0:T(8,128)(2,1)}, u32[]{:S(2)}, u32[]{:S(2)}) collective-permute-start(bf16[4096,128]{1,0:T(8,128)(2,1)} %pad_maximum_fusion.refs_2_.refs_4_.refs_6_), channel_id=1, source_target_pairs={{0,192},{1,193},{2,194},{3,195},{4,196},{5,197},{6,198},{7,199},{8... | collective-permute-start | bytes 3145736 | tf_op jit(solution)/shard_map/ppermute | solution.py:50
  74.1 8.5 %shard_map.84 = f32[8,224,256]{2,1,0:T(8,128)S(1)} custom-call(bf16[768,2048]{1,0:T(8,128)(2,1)S(1)} %copy-done, bf16[768,2048]{1,0:T(8,128)(2,1)} %collective-permute-done.refs_1_, bf16[256,2048]{1,0:T(8,128)(2,1)} %collective-permute-done.5.refs_2_, bf16[256,2048]{1,0:T(8,128)(2,1)} %collective-permute-done.6.refs_3_, ...), custom_call_target="tpu_custom_call" | custom-call | flops 1 | bytes 1 | tf_op jit(solution)/shard_map/pallas_call | solution.py:83
  88.7 8.6 %all-to-all-start.2 = ((f16[8,224,256]{2,1,0:T(8,128)(2,1)}), f16[8,224,256]{2,1,0:T(8,128)(2,1)}, u32[]{:S(2)}, u32[]{:S(2)}) async-start(f16[8,224,256]{2,1,0:T(8,128)(2,1)} %multiply_convert_fusion), calls=%async_computation.2 | async-start | bytes 1835008 | tf_op jit(solution)/shard_map/all_to_all | solution.py:54
  98.9 6.3 %shard_map.86 = f32[8,160,256]{2,1,0:T(8,128)S(1)} custom-call(bf16[768,2048]{1,0:T(8,128)(2,1)S(1)} %copy-done, bf16[768,2048]{1,0:T(8,128)(2,1)} %collective-permute-done.refs_1_, bf16[256,2048]{1,0:T(8,128)(2,1)} %collective-permute-done.5.refs_2_, bf16[256,2048]{1,0:T(8,128)(2,1)} %collective-permute-done.6.refs_3_, ...), custom_call_target="tpu_custom_call" | custom-call | flops 1 | bytes 1 | tf_op jit(solution)/shard_map/pallas_call | solution.py:83
  108.9 6.3 %shard_map.85 = f32[8,128,256]{2,1,0:T(8,128)S(1)} custom-call(bf16[256,2048]{1,0:T(8,128)(2,1)} %collective-permute-done.13.refs_0_, bf16[256,2048]{1,0:T(8,128)(2,1)} %collective-permute-done.14.refs_1_, bf16[4096,128]{1,0:T(8,128)(2,1)} %pad_maximum_fusion.refs_2_.refs_4_.refs_6_, bf16[4096,128]{1,0:T(8,128)(2,1)} %pad_maximum_fusion.1.refs_3_.refs_5_.refs_7_, ...), custom_call_target="tpu_custom_call" | custom-call | flops 1 | bytes 1 | tf_op jit(solution)/shard_map/pallas_call | solution.py:83
  115.2 6.5 %all-to-all-done.2 = f16[8,224,256]{2,1,0:T(8,128)(2,1)} async-done(((f16[8,224,256]{2,1,0:T(8,128)(2,1)}), f16[8,224,256]{2,1,0:T(8,128)(2,1)}, u32[]{:S(2)}, u32[]{:S(2)}) %all-to-all-start.2) | async-done | bytes 917536 | tf_op jit(solution)/shard_map/all_to_all | solution.py:54
  125.4 4.2 %collective-permute-done.17 = f16[8,128,128]{2,1,0:T(8,128)(2,1)S(1)} collective-permute-done((f16[8,128,128]{2,1,0:T(8,128)(2,1)S(1)}, f16[8,128,128]{2,1,0:T(8,128)(2,1)S(1)}, u32[]{:S(2)}, u32[]{:S(2)}) %collective-permute-start.17) | collective-permute-done | bytes 262176 | tf_op jit(solution)/shard_map/ppermute | solution.py:50
  130.7 6.8 %all-to-all-start.3 = ((f16[8,288,128]{2,1,0:T(8,128)(2,1)}), f16[8,288,128]{2,1,0:T(8,128)(2,1)S(1)}, u32[]{:S(2)}, u32[]{:S(2)}) async-start(f16[8,288,128]{2,1,0:T(8,128)(2,1)} %pad_maximum_fusion.2), calls=%async_computation.3 | async-start | bytes 1179648 | tf_op jit(solution)/shard_map/all_to_all | solution.py:54
  138.9 5.7 %collective-permute-done.15 = f32[480,128]{1,0:T(8,128)S(1)} collective-permute-done((f32[480,128]{1,0:T(8,128)S(1)}, f32[480,128]{1,0:T(8,128)S(1)}, u32[]{:S(2)}, u32[]{:S(2)}) %collective-permute-start.15) | collective-permute-done | bytes 245792 | tf_op jit(solution)/shard_map/ppermute | solution.py:50
  147.4 7.1 %all-to-all-done.3 = f16[8,288,128]{2,1,0:T(8,128)(2,1)S(1)} async-done(((f16[8,288,128]{2,1,0:T(8,128)(2,1)}), f16[8,288,128]{2,1,0:T(8,128)(2,1)S(1)}, u32[]{:S(2)}, u32[]{:S(2)}) %all-to-all-start.3) | async-done | bytes 589856 | tf_op jit(solution)/shard_map/all_to_all | solution.py:54
  158.0 2.9 %collective-permute-done.19.late_far_ref = f32[192,128]{1,0:T(8,128)S(1)} collective-permute-done((f32[192,128]{1,0:T(8,128)S(1)}, f32[192,128]{1,0:T(8,128)S(1)}, u32[]{:S(2)}, u32[]{:S(2)}) %collective-permute-start.19) | collective-permute-done | bytes 98336 | tf_op jit(solution)/shard_map/ppermute | solution.py:50
  163.4 4.8 %all-to-all-start.4 = ((f32[8,96,128]{2,1,0:T(8,128)}), f32[8,96,128]{2,1,0:T(8,128)S(1)}, u32[]{:S(2)}, u32[]{:S(2)}) async-start(f32[8,96,128]{2,1,0:T(8,128)} %shard_map.87), calls=%async_computation.4 | async-start | bytes 786432 | tf_op jit(solution)/shard_map/all_to_all | solution.py:54
  169.3 10.5 %all-to-all-done.4 = f32[8,96,128]{2,1,0:T(8,128)S(1)} async-done(((f32[8,96,128]{2,1,0:T(8,128)}), f32[8,96,128]{2,1,0:T(8,128)S(1)}, u32[]{:S(2)}, u32[]{:S(2)}) %all-to-all-start.4) | async-done | bytes 393248 | tf_op jit(solution)/shard_map/all_to_all | solution.py:54
  (114 shorter events, 43.6 us)
Async XLA Ops:
  0.0 11.8 %collective-permute-start = (bf16[768,2048]{1,0:T(8,128)(2,1)}, bf16[768,2048]{1,0:T(8,128)(2,1)}, u32[]{:S(2)}, u32[]{:S(2)}) collective-permute-start(bf16[768,2048]{1,0:T(8,128)(2,1)} %refs_0_.7), channel_id=1, source_target_pairs={{0,1},{1,0},{2,3},{3,2},{4,5},{5,4},{6,7},{7,6},{8,9},{9,8},{10,11... | collective-permute-start | bytes 9437192 | tf_op jit(solution)/shard_map/ppermute | solution.py:50
  2.5 8.2 %collective-permute-start.1 = (bf16[2048,128]{1,0:T(8,128)(2,1)S(1)}, bf16[2048,128]{1,0:T(8,128)(2,1)S(1)}, u32[]{:S(2)}, u32[]{:S(2)}) collective-permute-start(bf16[2048,128]{1,0:T(8,128)(2,1)S(1)} %get-tuple-element.50), channel_id=1, source_target_pairs={{0,1},{1,0},{2,3},{3,2},{4,5},{5,4},{6,7},{7,6},{8,9},{9,8},{10,11... | collective-permute-start | bytes 1572872 | tf_op jit(solution)/shard_map/ppermute | solution.py:50
  3.7 27.4 %collective-permute-start.5 = (bf16[256,2048]{1,0:T(8,128)(2,1)}, bf16[256,2048]{1,0:T(8,128)(2,1)}, u32[]{:S(2)}, u32[]{:S(2)}) collective-permute-start(bf16[256,2048]{1,0:T(8,128)(2,1)} %slice.33), channel_id=1, source_target_pairs={{0,32},{1,33},{2,34},{3,35},{4,36},{5,37},{6,38},{7,39},{8,40},{9,... | collective-permute-start | bytes 3145736 | tf_op jit(solution)/shard_map/ppermute | solution.py:50
  7.9 25.9 %collective-permute-start.4 = (bf16[4096,128]{1,0:T(8,128)(2,1)}, bf16[4096,128]{1,0:T(8,128)(2,1)}, u32[]{:S(2)}, u32[]{:S(2)}) collective-permute-start(bf16[4096,128]{1,0:T(8,128)(2,1)} %pad_maximum_fusion.1.refs_3_.refs_5_.refs_7_), channel_id=1, source_target_pairs={{0,192},{1,193},{2,194},{3,195},{4,196},{5,197},{6,198},{7,199},{8... | collective-permute-start | bytes 3145736 | tf_op jit(solution)/shard_map/ppermute | solution.py:50
  11.8 26.5 %collective-permute-start.2 = (bf16[4096,128]{1,0:T(8,128)(2,1)}, bf16[4096,128]{1,0:T(8,128)(2,1)}, u32[]{:S(2)}, u32[]{:S(2)}) collective-permute-start(bf16[4096,128]{1,0:T(8,128)(2,1)} %pad_maximum_fusion.refs_2_.refs_4_.refs_6_), channel_id=1, source_target_pairs={{0,64},{1,65},{2,66},{3,67},{4,68},{5,69},{6,70},{7,71},{8,72},{9,... | collective-permute-start | bytes 3145736 | tf_op jit(solution)/shard_map/ppermute | solution.py:50
  16.9 28.4 %all-to-all-start = ((f16[8,96,256]{2,1,0:T(8,128)(2,1)}), f16[8,96,256]{2,1,0:T(8,128)(2,1)S(1)}, u32[]{:S(2)}, u32[]{:S(2)}) async-start(f16[8,96,256]{2,1,0:T(8,128)(2,1)} %multiply_convert_fusion.2), calls=%async_computation | async-start | bytes 786432 | tf_op jit(solution)/shard_map/all_to_all | solution.py:54
  38.3 7.0 %collective-permute-start.6 = (bf16[256,2048]{1,0:T(8,128)(2,1)}, bf16[256,2048]{1,0:T(8,128)(2,1)}, u32[]{:S(2)}, u32[]{:S(2)}) collective-permute-start(bf16[256,2048]{1,0:T(8,128)(2,1)} %collective-permute-done.5.refs_2_), channel_id=1, source_target_pairs={{0,1},{1,0},{2,3},{3,2},{4,5},{5,4},{6,7},{7,6},{8,9},{9,8},{10,11... | collective-permute-start | bytes 3145736 | tf_op jit(solution)/shard_map/ppermute | solution.py:50
  39.4 27.4 %collective-permute-start.9 = (bf16[256,2048]{1,0:T(8,128)(2,1)}, bf16[256,2048]{1,0:T(8,128)(2,1)}, u32[]{:S(2)}, u32[]{:S(2)}) collective-permute-start(bf16[256,2048]{1,0:T(8,128)(2,1)} %slice.34), channel_id=1, source_target_pairs={{0,32},{1,33},{2,34},{3,35},{4,36},{5,37},{6,38},{7,39},{8,40},{9,... | collective-permute-start | bytes 3145736 | tf_op jit(solution)/shard_map/ppermute | solution.py:50
  42.0 26.8 %collective-permute-start.7 = (bf16[4096,128]{1,0:T(8,128)(2,1)}, bf16[4096,128]{1,0:T(8,128)(2,1)}, u32[]{:S(2)}, u32[]{:S(2)}) collective-permute-start(bf16[4096,128]{1,0:T(8,128)(2,1)} %collective-permute-done.2.refs_6_.refs_8_.refs_4_), channel_id=1, source_target_pairs={{0,64},{1,65},{2,66},{3,67},{4,68},{5,69},{6,70},{7,71},{8,72},{9,... | collective-permute-start | bytes 3145736 | tf_op jit(solution)/shard_map/ppermute | solution.py:50
  42.0 26.8 %collective-permute-start.8 = (bf16[4096,128]{1,0:T(8,128)(2,1)}, bf16[4096,128]{1,0:T(8,128)(2,1)}, u32[]{:S(2)}, u32[]{:S(2)}) collective-permute-start(bf16[4096,128]{1,0:T(8,128)(2,1)} %collective-permute-done.4.refs_7_.refs_9_.refs_5_), channel_id=1, source_target_pairs={{0,192},{1,193},{2,194},{3,195},{4,196},{5,197},{6,198},{7,199},{8... | collective-permute-start | bytes 3145736 | tf_op jit(solution)/shard_map/ppermute | solution.py:50
  52.9 32.0 %all-to-all-start.1 = ((f16[8,160,256]{2,1,0:T(8,128)(2,1)}), f16[8,160,256]{2,1,0:T(8,128)(2,1)}, u32[]{:S(2)}, u32[]{:S(2)}) async-start(f16[8,160,256]{2,1,0:T(8,128)(2,1)} %multiply_convert_fusion.1), calls=%async_computation.1 | async-start | bytes 1310720 | tf_op jit(solution)/shard_map/all_to_all | solution.py:54
  68.9 5.2 %collective-permute-start.10 = (bf16[256,2048]{1,0:T(8,128)(2,1)}, bf16[256,2048]{1,0:T(8,128)(2,1)S(1)}, u32[]{:S(2)}, u32[]{:S(2)}) collective-permute-start(bf16[256,2048]{1,0:T(8,128)(2,1)} %collective-permute-done.9.refs_4_), channel_id=1, source_target_pairs={{0,1},{1,0},{2,3},{3,2},{4,5},{5,4},{6,7},{7,6},{8,9},{9,8},{10,11... | collective-permute-start | bytes 3145736 | tf_op jit(solution)/shard_map/ppermute | solution.py:50
  70.0 27.4 %collective-permute-start.13 = (bf16[256,2048]{1,0:T(8,128)(2,1)}, bf16[256,2048]{1,0:T(8,128)(2,1)}, u32[]{:S(2)}, u32[]{:S(2)}) collective-permute-start(bf16[256,2048]{1,0:T(8,128)(2,1)} %slice.36), channel_id=1, source_target_pairs={{0,32},{1,33},{2,34},{3,35},{4,36},{5,37},{6,38},{7,39},{8,40},{9,... | collective-permute-start | bytes 3145736 | tf_op jit(solution)/shard_map/ppermute | solution.py:50
  70.8 26.8 %collective-permute-start.11 = (bf16[4096,128]{1,0:T(8,128)(2,1)}, bf16[4096,128]{1,0:T(8,128)(2,1)}, u32[]{:S(2)}, u32[]{:S(2)}) collective-permute-start(bf16[4096,128]{1,0:T(8,128)(2,1)} %pad_maximum_fusion.1.refs_3_.refs_5_.refs_7_), channel_id=1, source_target_pairs={{0,64},{1,65},{2,66},{3,67},{4,68},{5,69},{6,70},{7,71},{8,72},{9,... | collective-permute-start | bytes 3145736 | tf_op jit(solution)/shard_map/ppermute | solution.py:50
  70.8 26.8 %collective-permute-start.12 = (bf16[4096,128]{1,0:T(8,128)(2,1)}, bf16[4096,128]{1,0:T(8,128)(2,1)}, u32[]{:S(2)}, u32[]{:S(2)}) collective-permute-start(bf16[4096,128]{1,0:T(8,128)(2,1)} %pad_maximum_fusion.refs_2_.refs_4_.refs_6_), channel_id=1, source_target_pairs={{0,192},{1,193},{2,194},{3,195},{4,196},{5,197},{6,198},{7,199},{8... | collective-permute-start | bytes 3145736 | tf_op jit(solution)/shard_map/ppermute | solution.py:50
  88.7 33.0 %all-to-all-start.2 = ((f16[8,224,256]{2,1,0:T(8,128)(2,1)}), f16[8,224,256]{2,1,0:T(8,128)(2,1)}, u32[]{:S(2)}, u32[]{:S(2)}) async-start(f16[8,224,256]{2,1,0:T(8,128)(2,1)} %multiply_convert_fusion), calls=%async_computation.2 | async-start | bytes 1835008 | tf_op jit(solution)/shard_map/all_to_all | solution.py:54
  97.7 10.4 %collective-permute-start.14 = (bf16[256,2048]{1,0:T(8,128)(2,1)}, bf16[256,2048]{1,0:T(8,128)(2,1)}, u32[]{:S(2)}, u32[]{:S(2)}) collective-permute-start(bf16[256,2048]{1,0:T(8,128)(2,1)} %collective-permute-done.13.refs_0_), channel_id=1, source_target_pairs={{0,1},{1,0},{2,3},{3,2},{4,5},{5,4},{6,7},{7,6},{8,9},{9,8},{10,11... | collective-permute-start | bytes 3145736 | tf_op jit(solution)/shard_map/ppermute | solution.py:50
  107.0 17.2 %collective-permute-start.16 = (f16[8,160,128]{2,1,0:T(8,128)(2,1)}, f16[8,160,128]{2,1,0:T(8,128)(2,1)}, u32[]{:S(2)}, u32[]{:S(2)}) collective-permute-start(f16[8,160,128]{2,1,0:T(8,128)(2,1)} %multiply_convert_fusion.4), channel_id=1, source_target_pairs={{0,2},{1,3},{2,0},{3,1},{4,6},{5,7},{6,4},{7,5},{8,10},{9,11},{10,... | collective-permute-start | bytes 983048 | tf_op jit(solution)/shard_map/ppermute | solution.py:50
  123.1 6.5 %collective-permute-start.17 = (f16[8,128,128]{2,1,0:T(8,128)(2,1)S(1)}, f16[8,128,128]{2,1,0:T(8,128)(2,1)S(1)}, u32[]{:S(2)}, u32[]{:S(2)}) collective-permute-start(f16[8,128,128]{2,1,0:T(8,128)(2,1)S(1)} %multiply_convert_fusion.6), channel_id=1, source_target_pairs={{0,2},{1,3},{2,0},{3,1},{4,6},{5,7},{6,4},{7,5},{8,10},{9,11},{10,... | collective-permute-start | bytes 786440 | tf_op jit(solution)/shard_map/ppermute | solution.py:50
  130.7 23.8 %all-to-all-start.3 = ((f16[8,288,128]{2,1,0:T(8,128)(2,1)}), f16[8,288,128]{2,1,0:T(8,128)(2,1)S(1)}, u32[]{:S(2)}, u32[]{:S(2)}) async-start(f16[8,288,128]{2,1,0:T(8,128)(2,1)} %pad_maximum_fusion.2), calls=%async_computation.3 | async-start | bytes 1179648 | tf_op jit(solution)/shard_map/all_to_all | solution.py:54
  137.5 7.1 %collective-permute-start.15 = (f32[480,128]{1,0:T(8,128)S(1)}, f32[480,128]{1,0:T(8,128)S(1)}, u32[]{:S(2)}, u32[]{:S(2)}) collective-permute-start(f32[480,128]{1,0:T(8,128)S(1)} %constant_dynamic-slice_fusion), channel_id=1, source_target_pairs={{0,2},{1,3},{2,0},{3,1},{4,6},{5,7},{6,4},{7,5},{8,10},{9,11},{10,... | collective-permute-start | bytes 737288 | tf_op jit(solution)/shard_map/ppermute | solution.py:50
  144.7 13.3 %collective-permute-start.18 = (f32[192,128]{1,0:T(8,128)S(1)}, f32[192,128]{1,0:T(8,128)S(1)}, u32[]{:S(2)}, u32[]{:S(2)}) collective-permute-start(f32[192,128]{1,0:T(8,128)S(1)} %slice.44), channel_id=1, source_target_pairs={{0,32},{1,33},{2,34},{3,35},{4,36},{5,37},{6,38},{7,39},{8,40},{9,... | collective-permute-start | bytes 294920 | tf_op jit(solution)/shard_map/ppermute | solution.py:50
  154.7 6.2 %collective-permute-start.19 = (f32[192,128]{1,0:T(8,128)S(1)}, f32[192,128]{1,0:T(8,128)S(1)}, u32[]{:S(2)}, u32[]{:S(2)}) collective-permute-start(f32[192,128]{1,0:T(8,128)S(1)} %slice.45), channel_id=1, source_target_pairs={{0,32},{1,33},{2,34},{3,35},{4,36},{5,37},{6,38},{7,39},{8,40},{9,... | collective-permute-start | bytes 294920 | tf_op jit(solution)/shard_map/ppermute | solution.py:50
  163.4 16.3 %all-to-all-start.4 = ((f32[8,96,128]{2,1,0:T(8,128)}), f32[8,96,128]{2,1,0:T(8,128)S(1)}, u32[]{:S(2)}, u32[]{:S(2)}) async-start(f32[8,96,128]{2,1,0:T(8,128)} %shard_map.87), calls=%async_computation.4 | async-start | bytes 786432 | tf_op jit(solution)/shard_map/all_to_all | solution.py:54
  (19 other events, 203.5 us)

commit v3 on v2

--- a/solution.py
+++ b/solution.py
@@ -141,7 +141,7 @@
         return lax.dynamic_slice_in_dim(integrals, which * 256 + of_core * 128, 128, axis=1)
 
     x, y_high = lax.axis_index("occ") // NYH, lax.axis_index("occ") % NYH
-    shifts = [0, 3 - 2 * y_low, 2, 1 + 2 * y_low]
+    shifts = [0, 3 - 2 * y_low, 1 + 2 * y_low, 2]
     places = jnp.stack(
         [2 * ((x + shift) % NX) + (y_high + far) % NYH for shift in shifts for far in range(2)]
     ).astype(jnp.int32)
@@ -160,22 +160,22 @@
     cols = [b]
     in0 = half_precision(products(rows, cols, PLAN[0]), SCALE_CHIP)
     s0 = reduce_z(in0, SCALE_CHIP)
-    p1, m1, ay0, later, in0 = barrier((p1, m1, ay0, amplitudes, in0))
-    p2, m2, ay1 = send(p1, X_UP), send(m1, X_DOWN), send(later[256:512], Y_FAR)
-    far = send(ay0, CORE)
-    rows, cols = rows + [(ay0, far)], cols + [(p1, m1)]
+    later, in0 = barrier((amplitudes, in0))
+    a1, a2 = later[256:512], later[512:]
+    ay0, a1, b0, b1, in0 = barrier((ay0, a1, b[0], b[1], in0))
+    p2, m2, ay1 = send(b1, X_UP), send(b0, X_DOWN), send(a1, Y_FAR)
+    rows, cols = rows + [(ay0, send(ay0, CORE))], cols + [(p1, m1)]
     new, s0 = barrier((products(rows, cols, PLAN[1]), s0))
     in1 = half_precision(new, SCALE_CHIP)
     s1 = reduce_z(in1, SCALE_CHIP)
-    p2, m2, ay1, later, b0, b1, in1 = barrier((p2, m2, ay1, amplitudes, b[0], b[1], in1))
-    p3, m3, ay2 = send(b1, X_UP), send(b0, X_DOWN), send(later[512:], Y_FAR)
-    far = send(ay1, CORE)
-    rows, cols = rows + [(ay1, far)], cols + [(p2, m2)]
+    p2, m2, ay1, a2, p1, m1, in1 = barrier((p2, m2, ay1, a2, p1, m1, in1))
+    p3, m3, ay2 = send(p1, X_UP), send(m1, X_DOWN), send(a2, Y_FAR)
+    rows, cols = rows + [(ay1, send(ay1, CORE))], cols + [(m2, p2)]
     new, s1 = barrier((products(rows, cols, PLAN[2]), s1))
     in2 = half_precision(new, SCALE_CHIP)
     s2 = reduce_z(in2, SCALE_CHIP)
     p3, m3, ay2, in2 = barrier((p3, m3, ay2, in2))
-    cols = cols + [(m3, p3)]
+    cols = cols + [(p3, m3)]
     last = [
         products(rows, cols[3:], [(u, 0) for u, _ in PLAN[3]]),
         products([(ay2, send(ay2, CORE))], cols, [(0, q) for _, q in PLAN[4]]),

time: 182 us -> 176 us (0.967)
  waiting for transfers between devices: 57.5 us -> 53.7 us
  starting transfers between devices: 62.9 us -> 60.8 us
    ppermute x20, waiting for transfers between devices: 33.4 us -> 27 us  [send(): return lax.ppermute(block, AXES, route)]
    all_to_all x5, waiting for transfers between devices: 24.1 us -> 26.7 us  [over_z(): lax.all_to_all(pieces, AXES, 0, 0, axis_index_groups=Z_GROUPS, tiled=True)]
  transfers between devices with their start and end apart: 25 -> 25, of which waited for: 12 -> 13; matrix products, arithmetic and copies ran while one was open for 10% -> 10% of each run, Pallas kernels for 18% -> 18%
where the time goes in v3:
time: 176 us; the launch traced here: 174 us
  starting transfers between devices  60.8 us (35%)
  waiting for transfers between devices  53.7 us (31%)
  Pallas kernels  33.8 us (19%)
  other arithmetic  14.2 us (8%)
  local copies, waits for them, and re-layouts  11.2 us (6%)
    all_to_all x5, starting transfers between devices, over_z(): lax.all_to_all(pieces, AXES, 0, 0, axis_index_groups=Z_GROUPS, tiled=True)  35.8 us
    pallas_call x5, Pallas kernels, products(): pl.pallas_call(kernel, out_shape=jax.ShapeDtypeStruct((NZ, 32 * len(plan)...  31.9 us
    ppermute x20, waiting for transfers between devices, send(): return lax.ppermute(block, AXES, route)  27 us
    all_to_all x5, waiting for transfers between devices, over_z(): lax.all_to_all(pieces, AXES, 0, 0, axis_index_groups=Z_GROUPS, tiled=True)  26.7 us
    ppermute x20, starting transfers between devices, send(): return lax.ppermute(block, AXES, route)  25 us
    convert_element_type x7, other arithmetic, half_precision(): return (block * scale).astype(jnp.float16)  6.52 us
    unnamed x40, local copies, waits for them, and re-layouts  6.1 us
  transfers between devices with their start and end apart: 25, of which 13 were waited for; matrix products, arithmetic and copies ran while one was open for 10% of the time, Pallas kernels for 18%

profile of v3, /device:TPU:32, one launch (start us, length us, event | category | flops | bytes accessed | tf_op | source)
XLA Modules:
  0.0 174.2 jit_solution(1417963082173604391)
XLA Ops:
  3.6 3.2 %collective-permute-start.1 = (bf16[256,2048]{1,0:T(8,128)(2,1)}, bf16[256,2048]{1,0:T(8,128)(2,1)}, u32[]{:S(2)}, u32[]{:S(2)}) collective-permute-start(bf16[256,2048]{1,0:T(8,128)(2,1)} %slice.33), channel_id=1, source_target_pairs={{0,32},{1,33},{2,34},{3,35},{4,36},{5,37},{6,38},{7,39},{8,40},{9,... | collective-permute-start | bytes 3145736 | tf_op jit(solution)/shard_map/ppermute | solution.py:50
  12.2 4.3 %shard_map.82 = f32[8,96,256]{2,1,0:T(8,128)S(1)} custom-call(bf16[768,2048]{1,0:T(8,128)(2,1)S(1)} %copy-done, bf16[768,2048]{1,0:T(8,128)(2,1)} %collective-permute-done.refs_1_, bf16[4096,128]{1,0:T(8,128)(2,1)} %pad_maximum_fusion.refs_2_.refs_4_.refs_6_, bf16[4096,128]{1,0:T(8,128)(2,1)} %pad_maximum_fusion.1.refs_3_.refs_5_.refs_7_), custom_call_target="tpu_custom_call" | custom-call | flops 1 | bytes 1 | tf_op jit(solution)/shard_map/pallas_call | solution.py:83
  17.3 8.6 %all-to-all-start = ((f16[8,96,256]{2,1,0:T(8,128)(2,1)}), f16[8,96,256]{2,1,0:T(8,128)(2,1)S(1)}, u32[]{:S(2)}, u32[]{:S(2)}) async-start(f16[8,96,256]{2,1,0:T(8,128)(2,1)} %multiply_convert_fusion.2), calls=%async_computation | async-start | bytes 786432 | tf_op jit(solution)/shard_map/all_to_all | solution.py:54
  27.4 3.7 %collective-permute-done.1.refs_2_ = bf16[256,2048]{1,0:T(8,128)(2,1)} collective-permute-done((bf16[256,2048]{1,0:T(8,128)(2,1)}, bf16[256,2048]{1,0:T(8,128)(2,1)}, u32[]{:S(2)}, u32[]{:S(2)}) %collective-permute-start.1) | collective-permute-done | bytes 1048608 | tf_op jit(solution)/shard_map/ppermute | solution.py:50
  34.7 2.7 %collective-permute-start.9 = (bf16[256,2048]{1,0:T(8,128)(2,1)}, bf16[256,2048]{1,0:T(8,128)(2,1)}, u32[]{:S(2)}, u32[]{:S(2)}) collective-permute-start(bf16[256,2048]{1,0:T(8,128)(2,1)} %get-tuple-element.30), channel_id=1, source_target_pairs={{0,32},{1,33},{2,34},{3,35},{4,36},{5,37},{6,38},{7,39},{8,40},{9,... | collective-permute-start | bytes 3145736 | tf_op jit(solution)/shard_map/ppermute | solution.py:50
  39.0 6.5 %shard_map.83 = f32[8,160,256]{2,1,0:T(8,128)S(1)} custom-call(bf16[768,2048]{1,0:T(8,128)(2,1)S(1)} %copy-done, bf16[768,2048]{1,0:T(8,128)(2,1)} %collective-permute-done.refs_1_, bf16[256,2048]{1,0:T(8,128)(2,1)} %collective-permute-done.1.refs_2_, bf16[256,2048]{1,0:T(8,128)(2,1)} %collective-permute-done.4.refs_3_, ...), custom_call_target="tpu_custom_call" | custom-call | flops 1 | bytes 1 | tf_op jit(solution)/shard_map/pallas_call | solution.py:83
  46.6 7.1 %all-to-all-start.1 = ((f16[8,160,256]{2,1,0:T(8,128)(2,1)}), f16[8,160,256]{2,1,0:T(8,128)(2,1)}, u32[]{:S(2)}, u32[]{:S(2)}) async-start(f16[8,160,256]{2,1,0:T(8,128)(2,1)} %multiply_convert_fusion.1), calls=%async_computation.1 | async-start | bytes 1310720 | tf_op jit(solution)/shard_map/all_to_all | solution.py:54
  53.7 4.5 %collective-permute-done.7.refs_11_.refs_7_ = bf16[4096,128]{1,0:T(8,128)(2,1)} collective-permute-done((bf16[4096,128]{1,0:T(8,128)(2,1)}, bf16[4096,128]{1,0:T(8,128)(2,1)}, u32[]{:S(2)}, u32[]{:S(2)}) %collective-permute-start.7) | collective-permute-done | bytes 1048608 | tf_op jit(solution)/shard_map/ppermute | solution.py:50
  58.3 2.8 %collective-permute-done.9.refs_4_ = bf16[256,2048]{1,0:T(8,128)(2,1)} collective-permute-done((bf16[256,2048]{1,0:T(8,128)(2,1)}, bf16[256,2048]{1,0:T(8,128)(2,1)}, u32[]{:S(2)}, u32[]{:S(2)}) %collective-permute-start.9) | collective-permute-done | bytes 1048608 | tf_op jit(solution)/shard_map/ppermute | solution.py:50
  61.4 3.0 %collective-permute-start.12 = (bf16[4096,128]{1,0:T(8,128)(2,1)}, bf16[4096,128]{1,0:T(8,128)(2,1)}, u32[]{:S(2)}, u32[]{:S(2)}) collective-permute-start(bf16[4096,128]{1,0:T(8,128)(2,1)} %collective-permute-done.6.refs_7_.refs_9_.refs_5_), channel_id=1, source_target_pairs={{0,192},{1,193},{2,194},{3,195},{4,196},{5,197},{6,198},{7,199},{8... | collective-permute-start | bytes 3145736 | tf_op jit(solution)/shard_map/ppermute | solution.py:50
  64.3 3.2 %collective-permute-start.13 = (bf16[256,2048]{1,0:T(8,128)(2,1)}, bf16[256,2048]{1,0:T(8,128)(2,1)}, u32[]{:S(2)}, u32[]{:S(2)}) collective-permute-start(bf16[256,2048]{1,0:T(8,128)(2,1)} %get-tuple-element.38), channel_id=1, source_target_pairs={{0,32},{1,33},{2,34},{3,35},{4,36},{5,37},{6,38},{7,39},{8,40},{9,... | collective-permute-start | bytes 3145736 | tf_op jit(solution)/shard_map/ppermute | solution.py:50
  67.5 8.5 %shard_map.84 = f32[8,224,256]{2,1,0:T(8,128)S(1)} custom-call(bf16[768,2048]{1,0:T(8,128)(2,1)S(1)} %copy-done, bf16[768,2048]{1,0:T(8,128)(2,1)} %collective-permute-done.refs_1_, bf16[256,2048]{1,0:T(8,128)(2,1)} %collective-permute-done.1.refs_2_, bf16[256,2048]{1,0:T(8,128)(2,1)} %collective-permute-done.4.refs_3_, ...), custom_call_target="tpu_custom_call" | custom-call | flops 1 | bytes 1 | tf_op jit(solution)/shard_map/pallas_call | solution.py:83
  79.6 2.6 %multiply_convert_fusion = f16[8,224,256]{2,1,0:T(8,128)(2,1)} fusion(f32[8,224,256]{2,1,0:T(8,128)} %copy-done.1), kind=kLoop, calls=%fused_computation.1 | loop fusion | flops 917504 | bytes 2752512 | tf_op jit(solution)/shard_map/convert_element_type | solution.py:94
  82.2 8.6 %all-to-all-start.2 = ((f16[8,224,256]{2,1,0:T(8,128)(2,1)}), f16[8,224,256]{2,1,0:T(8,128)(2,1)}, u32[]{:S(2)}, u32[]{:S(2)}) async-start(f16[8,224,256]{2,1,0:T(8,128)(2,1)} %multiply_convert_fusion), calls=%async_computation.2 | async-start | bytes 1835008 | tf_op jit(solution)/shard_map/all_to_all | solution.py:54
  92.4 6.3 %shard_map.86 = f32[8,160,256]{2,1,0:T(8,128)S(1)} custom-call(bf16[768,2048]{1,0:T(8,128)(2,1)S(1)} %copy-done, bf16[768,2048]{1,0:T(8,128)(2,1)} %collective-permute-done.refs_1_, bf16[256,2048]{1,0:T(8,128)(2,1)} %collective-permute-done.1.refs_2_, bf16[256,2048]{1,0:T(8,128)(2,1)} %collective-permute-done.4.refs_3_, ...), custom_call_target="tpu_custom_call" | custom-call | flops 1 | bytes 1 | tf_op jit(solution)/shard_map/pallas_call | solution.py:83
  102.9 6.3 %shard_map.85 = f32[8,128,256]{2,1,0:T(8,128)S(1)} custom-call(bf16[256,2048]{1,0:T(8,128)(2,1)} %collective-permute-done.13.refs_0_, bf16[256,2048]{1,0:T(8,128)(2,1)} %collective-permute-done.14.refs_1_, bf16[4096,128]{1,0:T(8,128)(2,1)} %pad_maximum_fusion.refs_2_.refs_4_.refs_6_, bf16[4096,128]{1,0:T(8,128)(2,1)} %pad_maximum_fusion.1.refs_3_.refs_5_.refs_7_, ...), custom_call_target="tpu_custom_call" | custom-call | flops 1 | bytes 1 | tf_op jit(solution)/shard_map/pallas_call | solution.py:83
  109.3 5.9 %all-to-all-done.2 = f16[8,224,256]{2,1,0:T(8,128)(2,1)} async-done(((f16[8,224,256]{2,1,0:T(8,128)(2,1)}), f16[8,224,256]{2,1,0:T(8,128)(2,1)}, u32[]{:S(2)}, u32[]{:S(2)}) %all-to-all-start.2) | async-done | bytes 917536 | tf_op jit(solution)/shard_map/all_to_all | solution.py:54
  118.5 4.6 %collective-permute-done.17 = f16[8,128,128]{2,1,0:T(8,128)(2,1)S(1)} collective-permute-done((f16[8,128,128]{2,1,0:T(8,128)(2,1)S(1)}, f16[8,128,128]{2,1,0:T(8,128)(2,1)S(1)}, u32[]{:S(2)}, u32[]{:S(2)}) %collective-permute-start.17) | collective-permute-done | bytes 262176 | tf_op jit(solution)/shard_map/ppermute | solution.py:50
  124.1 6.8 %all-to-all-start.3 = ((f16[8,288,128]{2,1,0:T(8,128)(2,1)}), f16[8,288,128]{2,1,0:T(8,128)(2,1)S(1)}, u32[]{:S(2)}, u32[]{:S(2)}) async-start(f16[8,288,128]{2,1,0:T(8,128)(2,1)} %pad_maximum_fusion.2), calls=%async_computation.3 | async-start | bytes 1179648 | tf_op jit(solution)/shard_map/all_to_all | solution.py:54
  131.7 6.1 %collective-permute-done.15 = f32[480,128]{1,0:T(8,128)S(1)} collective-permute-done((f32[480,128]{1,0:T(8,128)S(1)}, f32[480,128]{1,0:T(8,128)S(1)}, u32[]{:S(2)}, u32[]{:S(2)}) %collective-permute-start.15) | collective-permute-done | bytes 245792 | tf_op jit(solution)/shard_map/ppermute | solution.py:50
  139.1 8.9 %all-to-all-done.3 = f16[8,288,128]{2,1,0:T(8,128)(2,1)S(1)} async-done(((f16[8,288,128]{2,1,0:T(8,128)(2,1)}), f16[8,288,128]{2,1,0:T(8,128)(2,1)S(1)}, u32[]{:S(2)}, u32[]{:S(2)}) %all-to-all-start.3) | async-done | bytes 589856 | tf_op jit(solution)/shard_map/all_to_all | solution.py:54
  149.9 4.4 %collective-permute-done.19.late_far_ref = f32[192,128]{1,0:T(8,128)S(1)} collective-permute-done((f32[192,128]{1,0:T(8,128)S(1)}, f32[192,128]{1,0:T(8,128)S(1)}, u32[]{:S(2)}, u32[]{:S(2)}) %collective-permute-start.19) | collective-permute-done | bytes 98336 | tf_op jit(solution)/shard_map/ppermute | solution.py:50
  156.9 4.8 %all-to-all-start.4 = ((f32[8,96,128]{2,1,0:T(8,128)}), f32[8,96,128]{2,1,0:T(8,128)S(1)}, u32[]{:S(2)}, u32[]{:S(2)}) async-start(f32[8,96,128]{2,1,0:T(8,128)} %shard_map.87), calls=%async_computation.4 | async-start | bytes 786432 | tf_op jit(solution)/shard_map/all_to_all | solution.py:54
  162.7 10.5 %all-to-all-done.4 = f32[8,96,128]{2,1,0:T(8,128)S(1)} async-done(((f32[8,96,128]{2,1,0:T(8,128)}), f32[8,96,128]{2,1,0:T(8,128)S(1)}, u32[]{:S(2)}, u32[]{:S(2)}) %all-to-all-start.4) | async-done | bytes 393248 | tf_op jit(solution)/shard_map/all_to_all | solution.py:54
  (113 shorter events, 40.1 us)
Async XLA Ops:
  0.0 12.2 %collective-permute-start = (bf16[768,2048]{1,0:T(8,128)(2,1)}, bf16[768,2048]{1,0:T(8,128)(2,1)}, u32[]{:S(2)}, u32[]{:S(2)}) collective-permute-start(bf16[768,2048]{1,0:T(8,128)(2,1)} %refs_0_.7), channel_id=1, source_target_pairs={{0,1},{1,0},{2,3},{3,2},{4,5},{5,4},{6,7},{7,6},{8,9},{9,8},{10,11... | collective-permute-start | bytes 9437192 | tf_op jit(solution)/shard_map/ppermute | solution.py:50
  2.5 6.9 %collective-permute-start.3 = (bf16[2048,128]{1,0:T(8,128)(2,1)S(1)}, bf16[2048,128]{1,0:T(8,128)(2,1)S(1)}, u32[]{:S(2)}, u32[]{:S(2)}) collective-permute-start(bf16[2048,128]{1,0:T(8,128)(2,1)S(1)} %get-tuple-element.56), channel_id=1, source_target_pairs={{0,1},{1,0},{2,3},{3,2},{4,5},{5,4},{6,7},{7,6},{8,9},{9,8},{10,11... | collective-permute-start | bytes 1572872 | tf_op jit(solution)/shard_map/ppermute | solution.py:50
  3.6 27.4 %collective-permute-start.1 = (bf16[256,2048]{1,0:T(8,128)(2,1)}, bf16[256,2048]{1,0:T(8,128)(2,1)}, u32[]{:S(2)}, u32[]{:S(2)}) collective-permute-start(bf16[256,2048]{1,0:T(8,128)(2,1)} %slice.33), channel_id=1, source_target_pairs={{0,32},{1,33},{2,34},{3,35},{4,36},{5,37},{6,38},{7,39},{8,40},{9,... | collective-permute-start | bytes 3145736 | tf_op jit(solution)/shard_map/ppermute | solution.py:50
  7.9 26.8 %collective-permute-start.5 = (bf16[4096,128]{1,0:T(8,128)(2,1)}, bf16[4096,128]{1,0:T(8,128)(2,1)}, u32[]{:S(2)}, u32[]{:S(2)}) collective-permute-start(bf16[4096,128]{1,0:T(8,128)(2,1)} %pad_maximum_fusion.refs_2_.refs_4_.refs_6_), channel_id=1, source_target_pairs={{0,64},{1,65},{2,66},{3,67},{4,68},{5,69},{6,70},{7,71},{8,72},{9,... | collective-permute-start | bytes 3145736 | tf_op jit(solution)/shard_map/ppermute | solution.py:50
  10.5 28.6 %collective-permute-start.6 = (bf16[4096,128]{1,0:T(8,128)(2,1)}, bf16[4096,128]{1,0:T(8,128)(2,1)}, u32[]{:S(2)}, u32[]{:S(2)}) collective-permute-start(bf16[4096,128]{1,0:T(8,128)(2,1)} %pad_maximum_fusion.1.refs_3_.refs_5_.refs_7_), channel_id=1, source_target_pairs={{0,192},{1,193},{2,194},{3,195},{4,196},{5,197},{6,198},{7,199},{8... | collective-permute-start | bytes 3145736 | tf_op jit(solution)/shard_map/ppermute | solution.py:50
  17.3 21.6 %all-to-all-start = ((f16[8,96,256]{2,1,0:T(8,128)(2,1)}), f16[8,96,256]{2,1,0:T(8,128)(2,1)S(1)}, u32[]{:S(2)}, u32[]{:S(2)}) async-start(f16[8,96,256]{2,1,0:T(8,128)(2,1)} %multiply_convert_fusion.2), calls=%async_computation | async-start | bytes 786432 | tf_op jit(solution)/shard_map/all_to_all | solution.py:54
  31.0 8.0 %collective-permute-start.4 = (bf16[256,2048]{1,0:T(8,128)(2,1)}, bf16[256,2048]{1,0:T(8,128)(2,1)}, u32[]{:S(2)}, u32[]{:S(2)}) collective-permute-start(bf16[256,2048]{1,0:T(8,128)(2,1)} %collective-permute-done.1.refs_2_), channel_id=1, source_target_pairs={{0,1},{1,0},{2,3},{3,2},{4,5},{5,4},{6,7},{7,6},{8,9},{9,8},{10,11... | collective-permute-start | bytes 3145736 | tf_op jit(solution)/shard_map/ppermute | solution.py:50
  31.0 27.1 %collective-permute-start.7 = (bf16[4096,128]{1,0:T(8,128)(2,1)}, bf16[4096,128]{1,0:T(8,128)(2,1)}, u32[]{:S(2)}, u32[]{:S(2)}) collective-permute-start(bf16[4096,128]{1,0:T(8,128)(2,1)} %pad_maximum_fusion.1.refs_3_.refs_5_.refs_7_), channel_id=1, source_target_pairs={{0,64},{1,65},{2,66},{3,67},{4,68},{5,69},{6,70},{7,71},{8,72},{9,... | collective-permute-start | bytes 3145736 | tf_op jit(solution)/shard_map/ppermute | solution.py:50
  32.5 25.7 %collective-permute-start.8 = (bf16[4096,128]{1,0:T(8,128)(2,1)}, bf16[4096,128]{1,0:T(8,128)(2,1)}, u32[]{:S(2)}, u32[]{:S(2)}) collective-permute-start(bf16[4096,128]{1,0:T(8,128)(2,1)} %pad_maximum_fusion.refs_2_.refs_4_.refs_6_), channel_id=1, source_target_pairs={{0,192},{1,193},{2,194},{3,195},{4,196},{5,197},{6,198},{7,199},{8... | collective-permute-start | bytes 3145736 | tf_op jit(solution)/shard_map/ppermute | solution.py:50
  34.7 26.4 %collective-permute-start.9 = (bf16[256,2048]{1,0:T(8,128)(2,1)}, bf16[256,2048]{1,0:T(8,128)(2,1)}, u32[]{:S(2)}, u32[]{:S(2)}) collective-permute-start(bf16[256,2048]{1,0:T(8,128)(2,1)} %get-tuple-element.30), channel_id=1, source_target_pairs={{0,32},{1,33},{2,34},{3,35},{4,36},{5,37},{6,38},{7,39},{8,40},{9,... | collective-permute-start | bytes 3145736 | tf_op jit(solution)/shard_map/ppermute | solution.py:50
  46.6 31.8 %all-to-all-start.1 = ((f16[8,160,256]{2,1,0:T(8,128)(2,1)}), f16[8,160,256]{2,1,0:T(8,128)(2,1)}, u32[]{:S(2)}, u32[]{:S(2)}) async-start(f16[8,160,256]{2,1,0:T(8,128)(2,1)} %multiply_convert_fusion.1), calls=%async_computation.1 | async-start | bytes 1310720 | tf_op jit(solution)/shard_map/all_to_all | solution.py:54
  61.1 6.4 %collective-permute-start.10 = (bf16[256,2048]{1,0:T(8,128)(2,1)}, bf16[256,2048]{1,0:T(8,128)(2,1)S(1)}, u32[]{:S(2)}, u32[]{:S(2)}) collective-permute-start(bf16[256,2048]{1,0:T(8,128)(2,1)} %collective-permute-done.9.refs_4_), channel_id=1, source_target_pairs={{0,1},{1,0},{2,3},{3,2},{4,5},{5,4},{6,7},{7,6},{8,9},{9,8},{10,11... | collective-permute-start | bytes 3145736 | tf_op jit(solution)/shard_map/ppermute | solution.py:50
  61.1 29.7 %collective-permute-start.11 = (bf16[4096,128]{1,0:T(8,128)(2,1)}, bf16[4096,128]{1,0:T(8,128)(2,1)}, u32[]{:S(2)}, u32[]{:S(2)}) collective-permute-start(bf16[4096,128]{1,0:T(8,128)(2,1)} %collective-permute-done.5.refs_6_.refs_8_.refs_4_), channel_id=1, source_target_pairs={{0,64},{1,65},{2,66},{3,67},{4,68},{5,69},{6,70},{7,71},{8,72},{9,... | collective-permute-start | bytes 3145736 | tf_op jit(solution)/shard_map/ppermute | solution.py:50
  61.4 29.4 %collective-permute-start.12 = (bf16[4096,128]{1,0:T(8,128)(2,1)}, bf16[4096,128]{1,0:T(8,128)(2,1)}, u32[]{:S(2)}, u32[]{:S(2)}) collective-permute-start(bf16[4096,128]{1,0:T(8,128)(2,1)} %collective-permute-done.6.refs_7_.refs_9_.refs_5_), channel_id=1, source_target_pairs={{0,192},{1,193},{2,194},{3,195},{4,196},{5,197},{6,198},{7,199},{8... | collective-permute-start | bytes 3145736 | tf_op jit(solution)/shard_map/ppermute | solution.py:50
  64.3 26.8 %collective-permute-start.13 = (bf16[256,2048]{1,0:T(8,128)(2,1)}, bf16[256,2048]{1,0:T(8,128)(2,1)}, u32[]{:S(2)}, u32[]{:S(2)}) collective-permute-start(bf16[256,2048]{1,0:T(8,128)(2,1)} %get-tuple-element.38), channel_id=1, source_target_pairs={{0,32},{1,33},{2,34},{3,35},{4,36},{5,37},{6,38},{7,39},{8,40},{9,... | collective-permute-start | bytes 3145736 | tf_op jit(solution)/shard_map/ppermute | solution.py:50
  82.2 33.0 %all-to-all-start.2 = ((f16[8,224,256]{2,1,0:T(8,128)(2,1)}), f16[8,224,256]{2,1,0:T(8,128)(2,1)}, u32[]{:S(2)}, u32[]{:S(2)}) async-start(f16[8,224,256]{2,1,0:T(8,128)(2,1)} %multiply_convert_fusion), calls=%async_computation.2 | async-start | bytes 1835008 | tf_op jit(solution)/shard_map/all_to_all | solution.py:54
  91.2 11.0 %collective-permute-start.14 = (bf16[256,2048]{1,0:T(8,128)(2,1)}, bf16[256,2048]{1,0:T(8,128)(2,1)}, u32[]{:S(2)}, u32[]{:S(2)}) collective-permute-start(bf16[256,2048]{1,0:T(8,128)(2,1)} %collective-permute-done.13.refs_0_), channel_id=1, source_target_pairs={{0,1},{1,0},{2,3},{3,2},{4,5},{5,4},{6,7},{7,6},{8,9},{9,8},{10,11... | collective-permute-start | bytes 3145736 | tf_op jit(solution)/shard_map/ppermute | solution.py:50
  100.6 16.8 %collective-permute-start.16 = (f16[8,160,128]{2,1,0:T(8,128)(2,1)}, f16[8,160,128]{2,1,0:T(8,128)(2,1)}, u32[]{:S(2)}, u32[]{:S(2)}) collective-permute-start(f16[8,160,128]{2,1,0:T(8,128)(2,1)} %multiply_convert_fusion.4), channel_id=1, source_target_pairs={{0,2},{1,3},{2,0},{3,1},{4,6},{5,7},{6,4},{7,5},{8,10},{9,11},{10,... | collective-permute-start | bytes 983048 | tf_op jit(solution)/shard_map/ppermute | solution.py:50
  116.6 6.5 %collective-permute-start.17 = (f16[8,128,128]{2,1,0:T(8,128)(2,1)S(1)}, f16[8,128,128]{2,1,0:T(8,128)(2,1)S(1)}, u32[]{:S(2)}, u32[]{:S(2)}) collective-permute-start(f16[8,128,128]{2,1,0:T(8,128)(2,1)S(1)} %multiply_convert_fusion.6), channel_id=1, source_target_pairs={{0,2},{1,3},{2,0},{3,1},{4,6},{5,7},{6,4},{7,5},{8,10},{9,11},{10,... | collective-permute-start | bytes 786440 | tf_op jit(solution)/shard_map/ppermute | solution.py:50
  124.1 23.8 %all-to-all-start.3 = ((f16[8,288,128]{2,1,0:T(8,128)(2,1)}), f16[8,288,128]{2,1,0:T(8,128)(2,1)S(1)}, u32[]{:S(2)}, u32[]{:S(2)}) async-start(f16[8,288,128]{2,1,0:T(8,128)(2,1)} %pad_maximum_fusion.2), calls=%async_computation.3 | async-start | bytes 1179648 | tf_op jit(solution)/shard_map/all_to_all | solution.py:54
  131.0 6.8 %collective-permute-start.15 = (f32[480,128]{1,0:T(8,128)S(1)}, f32[480,128]{1,0:T(8,128)S(1)}, u32[]{:S(2)}, u32[]{:S(2)}) collective-permute-start(f32[480,128]{1,0:T(8,128)S(1)} %constant_dynamic-slice_fusion), channel_id=1, source_target_pairs={{0,2},{1,3},{2,0},{3,1},{4,6},{5,7},{6,4},{7,5},{8,10},{9,11},{10,... | collective-permute-start | bytes 737288 | tf_op jit(solution)/shard_map/ppermute | solution.py:50
  137.9 12.0 %collective-permute-start.18 = (f32[192,128]{1,0:T(8,128)S(1)}, f32[192,128]{1,0:T(8,128)S(1)}, u32[]{:S(2)}, u32[]{:S(2)}) collective-permute-start(f32[192,128]{1,0:T(8,128)S(1)} %slice.44), channel_id=1, source_target_pairs={{0,32},{1,33},{2,34},{3,35},{4,36},{5,37},{6,38},{7,39},{8,40},{9,... | collective-permute-start | bytes 294920 | tf_op jit(solution)/shard_map/ppermute | solution.py:50
  148.1 6.2 %collective-permute-start.19 = (f32[192,128]{1,0:T(8,128)S(1)}, f32[192,128]{1,0:T(8,128)S(1)}, u32[]{:S(2)}, u32[]{:S(2)}) collective-permute-start(f32[192,128]{1,0:T(8,128)S(1)} %slice.45), channel_id=1, source_target_pairs={{0,32},{1,33},{2,34},{3,35},{4,36},{5,37},{6,38},{7,39},{8,40},{9,... | collective-permute-start | bytes 294920 | tf_op jit(solution)/shard_map/ppermute | solution.py:50
  156.9 16.3 %all-to-all-start.4 = ((f32[8,96,128]{2,1,0:T(8,128)}), f32[8,96,128]{2,1,0:T(8,128)S(1)}, u32[]{:S(2)}, u32[]{:S(2)}) async-start(f32[8,96,128]{2,1,0:T(8,128)} %shard_map.87), calls=%async_computation.4 | async-start | bytes 786432 | tf_op jit(solution)/shard_map/all_to_all | solution.py:54
  (19 other events, 204.3 us)

commit v4 on v3

--- a/solution.py
+++ b/solution.py
@@ -94,8 +94,12 @@
     return (block * scale).astype(jnp.float16)
 
 
+def summed(got, scale):
+    return jnp.sum(got.astype(jnp.float32), axis=0) * (1.0 / scale)
+
+
 def reduce_z(batch, scale):
-    return jnp.sum(over_z(batch).astype(jnp.float32), axis=0) * (1.0 / scale)
+    return summed(over_z(batch), scale)
 
 
 def slots_of(places, early, late, early_far, late_far):
@@ -167,26 +171,29 @@
     rows, cols = rows + [(ay0, send(ay0, CORE))], cols + [(p1, m1)]
     new, s0 = barrier((products(rows, cols, PLAN[1]), s0))
     in1 = half_precision(new, SCALE_CHIP)
-    s1 = reduce_z(in1, SCALE_CHIP)
+    got1 = over_z(in1)
     p2, m2, ay1, a2, p1, m1, in1 = barrier((p2, m2, ay1, a2, p1, m1, in1))
     p3, m3, ay2 = send(p1, X_UP), send(m1, X_DOWN), send(a2, Y_FAR)
     rows, cols = rows + [(ay1, send(ay1, CORE))], cols + [(m2, p2)]
-    new, s1 = barrier((products(rows, cols, PLAN[2]), s1))
+    new, got1 = barrier((products(rows, cols, PLAN[2]), got1))
     in2 = half_precision(new, SCALE_CHIP)
-    s2 = reduce_z(in2, SCALE_CHIP)
+    got2 = over_z(in2)
     p3, m3, ay2, in2 = barrier((p3, m3, ay2, in2))
     cols = cols + [(p3, m3)]
     last = [
         products(rows, cols[3:], [(u, 0) for u, _ in PLAN[3]]),
         products([(ay2, send(ay2, CORE))], cols, [(0, q) for _, q in PLAN[4]]),
     ]
-    last[1], s2 = barrier((last[1], s2))
-    met = [send(half_precision(neighbours(part), SCALE_CHIP), Y_NEAR) for part in last]
+    leaving = [half_precision(neighbours(part), SCALE_CHIP) for part in last]
+    met = send(leaving[0], Y_NEAR)
+    leaving[1], got2, met = barrier((leaving[1], got2, met))
+    met = [met, send(leaving[1], Y_NEAR)]
     pair = [
         half_precision(mine(part) + got.astype(jnp.float32) * (1.0 / SCALE_CHIP), SCALE_PAIR)
         for part, got in zip(last, met)
     ]
     late = reduce_z(jnp.concatenate(pair, axis=1), SCALE_PAIR)
+    s1, s2 = summed(got1, SCALE_CHIP), summed(got2, SCALE_CHIP)
     early = jnp.concatenate([s0, s1[:96], s2[:96], s1[96:], s2[96:]], axis=0)
     early = mine(early) + send(neighbours(early), Y_NEAR)
     early_far, late_far = send(early[288:], Y_FAR), send(late[96:], Y_FAR)

time: 176 us -> 172 us (0.977)
  waiting for transfers between devices: 53.7 us -> 50.3 us
  starting transfers between devices: 60.8 us -> 63.1 us
    all_to_all x5, waiting for transfers between devices: 26.7 us -> 23.8 us  [over_z(): lax.all_to_all(pieces, AXES, 0, 0, axis_index_groups=Z_GROUPS, tiled=True)]
    ppermute x20, starting transfers between devices: 25 us -> 27.3 us  [send(): return lax.ppermute(block, AXES, route)]
  transfers between devices with their start and end apart: 25 -> 25, of which waited for: 13 -> 14; matrix products, arithmetic and copies ran while one was open for 10% -> 9% of each run, Pallas kernels for 18% -> 19%
where the time goes in v4:
time: 172 us; the launch traced here: 171 us
  starting transfers between devices  63.1 us (37%)
  waiting for transfers between devices  50.3 us (29%)
  Pallas kernels  34 us (20%)
  other arithmetic  12.5 us (7%)
  local copies, waits for them, and re-layouts  11.1 us (6%)
    all_to_all x5, starting transfers between devices, over_z(): lax.all_to_all(pieces, AXES, 0, 0, axis_index_groups=Z_GROUPS, tiled=True)  35.8 us
    pallas_call x5, Pallas kernels, products(): pl.pallas_call(kernel, out_shape=jax.ShapeDtypeStruct((NZ, 32 * len(plan)...  32.1 us
    ppermute x20, starting transfers between devices, send(): return lax.ppermute(block, AXES, route)  27.3 us
    ppermute x20, waiting for transfers between devices, send(): return lax.ppermute(block, AXES, route)  26.6 us
    all_to_all x5, waiting for transfers between devices, over_z(): lax.all_to_all(pieces, AXES, 0, 0, axis_index_groups=Z_GROUPS, tiled=True)  23.8 us
    unnamed x40, local copies, waits for them, and re-layouts  5.97 us
    convert_element_type x7, other arithmetic, half_precision(): return (block * scale).astype(jnp.float16)  4.83 us
  transfers between devices with their start and end apart: 25, of which 14 were waited for; matrix products, arithmetic and copies ran while one was open for 9% of the time, Pallas kernels for 19%

profile of v4, /device:TPU:32, one launch (start us, length us, event | category | flops | bytes accessed | tf_op | source)
XLA Modules:
  0.0 171.4 jit_solution(2453254827902767507)
XLA Ops:
  3.6 3.2 %collective-permute-start.1 = (bf16[256,2048]{1,0:T(8,128)(2,1)}, bf16[256,2048]{1,0:T(8,128)(2,1)}, u32[]{:S(2)}, u32[]{:S(2)}) collective-permute-start(bf16[256,2048]{1,0:T(8,128)(2,1)} %slice.33), channel_id=1, source_target_pairs={{0,32},{1,33},{2,34},{3,35},{4,36},{5,37},{6,38},{7,39},{8,40},{9,... | collective-permute-start | bytes 3145736 | tf_op jit(solution)/shard_map/ppermute | solution.py:50
  12.2 4.3 %shard_map.82 = f32[8,96,256]{2,1,0:T(8,128)S(1)} custom-call(bf16[768,2048]{1,0:T(8,128)(2,1)S(1)} %copy-done, bf16[768,2048]{1,0:T(8,128)(2,1)} %collective-permute-done.refs_1_, bf16[4096,128]{1,0:T(8,128)(2,1)} %pad_maximum_fusion.refs_2_.refs_4_.refs_6_, bf16[4096,128]{1,0:T(8,128)(2,1)} %pad_maximum_fusion.1.refs_3_.refs_5_.refs_7_), custom_call_target="tpu_custom_call" | custom-call | flops 1 | bytes 1 | tf_op jit(solution)/shard_map/pallas_call | solution.py:83
  17.3 8.6 %all-to-all-start = ((f16[8,96,256]{2,1,0:T(8,128)(2,1)}), f16[8,96,256]{2,1,0:T(8,128)(2,1)S(1)}, u32[]{:S(2)}, u32[]{:S(2)}) async-start(f16[8,96,256]{2,1,0:T(8,128)(2,1)} %multiply_convert_fusion.2), calls=%async_computation | async-start | bytes 786432 | tf_op jit(solution)/shard_map/all_to_all | solution.py:54
  27.4 3.7 %collective-permute-done.1.refs_2_ = bf16[256,2048]{1,0:T(8,128)(2,1)} collective-permute-done((bf16[256,2048]{1,0:T(8,128)(2,1)}, bf16[256,2048]{1,0:T(8,128)(2,1)}, u32[]{:S(2)}, u32[]{:S(2)}) %collective-permute-start.1) | collective-permute-done | bytes 1048608 | tf_op jit(solution)/shard_map/ppermute | solution.py:50
  34.7 2.7 %collective-permute-start.9 = (bf16[256,2048]{1,0:T(8,128)(2,1)}, bf16[256,2048]{1,0:T(8,128)(2,1)}, u32[]{:S(2)}, u32[]{:S(2)}) collective-permute-start(bf16[256,2048]{1,0:T(8,128)(2,1)} %get-tuple-element.31), channel_id=1, source_target_pairs={{0,32},{1,33},{2,34},{3,35},{4,36},{5,37},{6,38},{7,39},{8,40},{9,... | collective-permute-start | bytes 3145736 | tf_op jit(solution)/shard_map/ppermute | solution.py:50
  39.0 6.5 %shard_map.83 = f32[8,160,256]{2,1,0:T(8,128)S(1)} custom-call(bf16[768,2048]{1,0:T(8,128)(2,1)S(1)} %copy-done, bf16[768,2048]{1,0:T(8,128)(2,1)} %collective-permute-done.refs_1_, bf16[256,2048]{1,0:T(8,128)(2,1)} %collective-permute-done.1.refs_2_, bf16[256,2048]{1,0:T(8,128)(2,1)} %collective-permute-done.4.refs_3_, ...), custom_call_target="tpu_custom_call" | custom-call | flops 1 | bytes 1 | tf_op jit(solution)/shard_map/pallas_call | solution.py:83
  46.6 7.1 %all-to-all-start.1 = ((f16[8,160,256]{2,1,0:T(8,128)(2,1)}), f16[8,160,256]{2,1,0:T(8,128)(2,1)}, u32[]{:S(2)}, u32[]{:S(2)}) async-start(f16[8,160,256]{2,1,0:T(8,128)(2,1)} %multiply_convert_fusion.1), calls=%async_computation.1 | async-start | bytes 1310720 | tf_op jit(solution)/shard_map/all_to_all | solution.py:54
  53.7 4.4 %collective-permute-done.7.refs_11_.refs_7_ = bf16[4096,128]{1,0:T(8,128)(2,1)} collective-permute-done((bf16[4096,128]{1,0:T(8,128)(2,1)}, bf16[4096,128]{1,0:T(8,128)(2,1)}, u32[]{:S(2)}, u32[]{:S(2)}) %collective-permute-start.7) | collective-permute-done | bytes 1048608 | tf_op jit(solution)/shard_map/ppermute | solution.py:50
  58.3 2.8 %collective-permute-done.9.refs_4_ = bf16[256,2048]{1,0:T(8,128)(2,1)} collective-permute-done((bf16[256,2048]{1,0:T(8,128)(2,1)}, bf16[256,2048]{1,0:T(8,128)(2,1)}, u32[]{:S(2)}, u32[]{:S(2)}) %collective-permute-start.9) | collective-permute-done | bytes 1048608 | tf_op jit(solution)/shard_map/ppermute | solution.py:50
  61.4 3.0 %collective-permute-start.12 = (bf16[4096,128]{1,0:T(8,128)(2,1)}, bf16[4096,128]{1,0:T(8,128)(2,1)}, u32[]{:S(2)}, u32[]{:S(2)}) collective-permute-start(bf16[4096,128]{1,0:T(8,128)(2,1)} %collective-permute-done.6.refs_7_.refs_9_.refs_5_), channel_id=1, source_target_pairs={{0,192},{1,193},{2,194},{3,195},{4,196},{5,197},{6,198},{7,199},{8... | collective-permute-start | bytes 3145736 | tf_op jit(solution)/shard_map/ppermute | solution.py:50
  64.3 3.2 %collective-permute-start.13 = (bf16[256,2048]{1,0:T(8,128)(2,1)}, bf16[256,2048]{1,0:T(8,128)(2,1)}, u32[]{:S(2)}, u32[]{:S(2)}) collective-permute-start(bf16[256,2048]{1,0:T(8,128)(2,1)} %get-tuple-element.39), channel_id=1, source_target_pairs={{0,32},{1,33},{2,34},{3,35},{4,36},{5,37},{6,38},{7,39},{8,40},{9,... | collective-permute-start | bytes 3145736 | tf_op jit(solution)/shard_map/ppermute | solution.py:50
  67.5 8.5 %shard_map.84 = f32[8,224,256]{2,1,0:T(8,128)S(1)} custom-call(bf16[768,2048]{1,0:T(8,128)(2,1)S(1)} %copy-done, bf16[768,2048]{1,0:T(8,128)(2,1)} %collective-permute-done.refs_1_, bf16[256,2048]{1,0:T(8,128)(2,1)} %collective-permute-done.1.refs_2_, bf16[256,2048]{1,0:T(8,128)(2,1)} %collective-permute-done.4.refs_3_, ...), custom_call_target="tpu_custom_call" | custom-call | flops 1 | bytes 1 | tf_op jit(solution)/shard_map/pallas_call | solution.py:83
  78.3 2.6 %multiply_convert_fusion = f16[8,224,256]{2,1,0:T(8,128)(2,1)} fusion(f32[8,224,256]{2,1,0:T(8,128)} %copy-done.1), kind=kLoop, calls=%fused_computation.1 | loop fusion | flops 917504 | bytes 2752512 | tf_op jit(solution)/shard_map/convert_element_type | solution.py:94
  81.0 8.6 %all-to-all-start.2 = ((f16[8,224,256]{2,1,0:T(8,128)(2,1)}), f16[8,224,256]{2,1,0:T(8,128)(2,1)}, u32[]{:S(2)}, u32[]{:S(2)}) async-start(f16[8,224,256]{2,1,0:T(8,128)(2,1)} %multiply_convert_fusion), calls=%async_computation.2 | async-start | bytes 1835008 | tf_op jit(solution)/shard_map/all_to_all | solution.py:54
  92.4 6.3 %shard_map.86 = f32[8,160,256]{2,1,0:T(8,128)S(1)} custom-call(bf16[768,2048]{1,0:T(8,128)(2,1)S(1)} %copy-done, bf16[768,2048]{1,0:T(8,128)(2,1)} %collective-permute-done.refs_1_, bf16[256,2048]{1,0:T(8,128)(2,1)} %collective-permute-done.1.refs_2_, bf16[256,2048]{1,0:T(8,128)(2,1)} %collective-permute-done.4.refs_3_, ...), custom_call_target="tpu_custom_call" | custom-call | flops 1 | bytes 1 | tf_op jit(solution)/shard_map/pallas_call | solution.py:83
  102.7 6.5 %shard_map.85 = f32[8,128,256]{2,1,0:T(8,128)S(1)} custom-call(bf16[256,2048]{1,0:T(8,128)(2,1)} %collective-permute-done.13.refs_0_, bf16[256,2048]{1,0:T(8,128)(2,1)} %collective-permute-done.14.refs_1_, bf16[4096,128]{1,0:T(8,128)(2,1)} %pad_maximum_fusion.refs_2_.refs_4_.refs_6_, bf16[4096,128]{1,0:T(8,128)(2,1)} %pad_maximum_fusion.1.refs_3_.refs_5_.refs_7_, ...), custom_call_target="tpu_custom_call" | custom-call | flops 1 | bytes 1 | tf_op jit(solution)/shard_map/pallas_call | solution.py:83
  110.0 3.9 %all-to-all-done.2 = f16[8,224,256]{2,1,0:T(8,128)(2,1)} async-done(((f16[8,224,256]{2,1,0:T(8,128)(2,1)}), f16[8,224,256]{2,1,0:T(8,128)(2,1)}, u32[]{:S(2)}, u32[]{:S(2)}) %all-to-all-start.2) | async-done | bytes 917536 | tf_op jit(solution)/shard_map/all_to_all | solution.py:54
  116.8 3.5 %collective-permute-done.17 = f16[8,128,128]{2,1,0:T(8,128)(2,1)S(1)} collective-permute-done((f16[8,128,128]{2,1,0:T(8,128)(2,1)S(1)}, f16[8,128,128]{2,1,0:T(8,128)(2,1)S(1)}, u32[]{:S(2)}, u32[]{:S(2)}) %collective-permute-start.17) | collective-permute-done | bytes 262176 | tf_op jit(solution)/shard_map/ppermute | solution.py:50
  121.4 6.8 %all-to-all-start.3 = ((f16[8,288,128]{2,1,0:T(8,128)(2,1)}), f16[8,288,128]{2,1,0:T(8,128)(2,1)S(1)}, u32[]{:S(2)}, u32[]{:S(2)}) async-start(f16[8,288,128]{2,1,0:T(8,128)(2,1)} %pad_maximum_fusion.2), calls=%async_computation.3 | async-start | bytes 1179648 | tf_op jit(solution)/shard_map/all_to_all | solution.py:54
  129.4 5.7 %collective-permute-done.16 = f32[480,128]{1,0:T(8,128)S(1)} collective-permute-done((f32[480,128]{1,0:T(8,128)S(1)}, f32[480,128]{1,0:T(8,128)S(1)}, u32[]{:S(2)}, u32[]{:S(2)}) %collective-permute-start.16) | collective-permute-done | bytes 245792 | tf_op jit(solution)/shard_map/ppermute | solution.py:50
  137.4 7.9 %all-to-all-done.3 = f16[8,288,128]{2,1,0:T(8,128)(2,1)S(1)} async-done(((f16[8,288,128]{2,1,0:T(8,128)(2,1)}), f16[8,288,128]{2,1,0:T(8,128)(2,1)S(1)}, u32[]{:S(2)}, u32[]{:S(2)}) %all-to-all-start.3) | async-done | bytes 589856 | tf_op jit(solution)/shard_map/all_to_all | solution.py:54
  148.1 3.5 %collective-permute-done.19.late_far_ref = f32[192,128]{1,0:T(8,128)S(1)} collective-permute-done((f32[192,128]{1,0:T(8,128)S(1)}, f32[192,128]{1,0:T(8,128)S(1)}, u32[]{:S(2)}, u32[]{:S(2)}) %collective-permute-start.19) | collective-permute-done | bytes 98336 | tf_op jit(solution)/shard_map/ppermute | solution.py:50
  154.2 4.8 %all-to-all-start.4 = ((f32[8,96,128]{2,1,0:T(8,128)}), f32[8,96,128]{2,1,0:T(8,128)S(1)}, u32[]{:S(2)}, u32[]{:S(2)}) async-start(f32[8,96,128]{2,1,0:T(8,128)} %shard_map.87), calls=%async_computation.4 | async-start | bytes 786432 | tf_op jit(solution)/shard_map/all_to_all | solution.py:54
  160.0 10.5 %all-to-all-done.4 = f32[8,96,128]{2,1,0:T(8,128)S(1)} async-done(((f32[8,96,128]{2,1,0:T(8,128)}), f32[8,96,128]{2,1,0:T(8,128)S(1)}, u32[]{:S(2)}, u32[]{:S(2)}) %all-to-all-start.4) | async-done | bytes 393248 | tf_op jit(solution)/shard_map/all_to_all | solution.py:54
  (113 shorter events, 42.5 us)
Async XLA Ops:
  0.0 12.2 %collective-permute-start = (bf16[768,2048]{1,0:T(8,128)(2,1)}, bf16[768,2048]{1,0:T(8,128)(2,1)}, u32[]{:S(2)}, u32[]{:S(2)}) collective-permute-start(bf16[768,2048]{1,0:T(8,128)(2,1)} %refs_0_.7), channel_id=1, source_target_pairs={{0,1},{1,0},{2,3},{3,2},{4,5},{5,4},{6,7},{7,6},{8,9},{9,8},{10,11... | collective-permute-start | bytes 9437192 | tf_op jit(solution)/shard_map/ppermute | solution.py:50
  2.5 6.9 %collective-permute-start.3 = (bf16[2048,128]{1,0:T(8,128)(2,1)S(1)}, bf16[2048,128]{1,0:T(8,128)(2,1)S(1)}, u32[]{:S(2)}, u32[]{:S(2)}) collective-permute-start(bf16[2048,128]{1,0:T(8,128)(2,1)S(1)} %get-tuple-element.58), channel_id=1, source_target_pairs={{0,1},{1,0},{2,3},{3,2},{4,5},{5,4},{6,7},{7,6},{8,9},{9,8},{10,11... | collective-permute-start | bytes 1572872 | tf_op jit(solution)/shard_map/ppermute | solution.py:50
  3.6 27.4 %collective-permute-start.1 = (bf16[256,2048]{1,0:T(8,128)(2,1)}, bf16[256,2048]{1,0:T(8,128)(2,1)}, u32[]{:S(2)}, u32[]{:S(2)}) collective-permute-start(bf16[256,2048]{1,0:T(8,128)(2,1)} %slice.33), channel_id=1, source_target_pairs={{0,32},{1,33},{2,34},{3,35},{4,36},{5,37},{6,38},{7,39},{8,40},{9,... | collective-permute-start | bytes 3145736 | tf_op jit(solution)/shard_map/ppermute | solution.py:50
  7.9 26.8 %collective-permute-start.5 = (bf16[4096,128]{1,0:T(8,128)(2,1)}, bf16[4096,128]{1,0:T(8,128)(2,1)}, u32[]{:S(2)}, u32[]{:S(2)}) collective-permute-start(bf16[4096,128]{1,0:T(8,128)(2,1)} %pad_maximum_fusion.refs_2_.refs_4_.refs_6_), channel_id=1, source_target_pairs={{0,64},{1,65},{2,66},{3,67},{4,68},{5,69},{6,70},{7,71},{8,72},{9,... | collective-permute-start | bytes 3145736 | tf_op jit(solution)/shard_map/ppermute | solution.py:50
  10.5 28.6 %collective-permute-start.6 = (bf16[4096,128]{1,0:T(8,128)(2,1)}, bf16[4096,128]{1,0:T(8,128)(2,1)}, u32[]{:S(2)}, u32[]{:S(2)}) collective-permute-start(bf16[4096,128]{1,0:T(8,128)(2,1)} %pad_maximum_fusion.1.refs_3_.refs_5_.refs_7_), channel_id=1, source_target_pairs={{0,192},{1,193},{2,194},{3,195},{4,196},{5,197},{6,198},{7,199},{8... | collective-permute-start | bytes 3145736 | tf_op jit(solution)/shard_map/ppermute | solution.py:50
  17.3 21.6 %all-to-all-start = ((f16[8,96,256]{2,1,0:T(8,128)(2,1)}), f16[8,96,256]{2,1,0:T(8,128)(2,1)S(1)}, u32[]{:S(2)}, u32[]{:S(2)}) async-start(f16[8,96,256]{2,1,0:T(8,128)(2,1)} %multiply_convert_fusion.2), calls=%async_computation | async-start | bytes 786432 | tf_op jit(solution)/shard_map/all_to_all | solution.py:54
  31.0 8.0 %collective-permute-start.4 = (bf16[256,2048]{1,0:T(8,128)(2,1)}, bf16[256,2048]{1,0:T(8,128)(2,1)}, u32[]{:S(2)}, u32[]{:S(2)}) collective-permute-start(bf16[256,2048]{1,0:T(8,128)(2,1)} %collective-permute-done.1.refs_2_), channel_id=1, source_target_pairs={{0,1},{1,0},{2,3},{3,2},{4,5},{5,4},{6,7},{7,6},{8,9},{9,8},{10,11... | collective-permute-start | bytes 3145736 | tf_op jit(solution)/shard_map/ppermute | solution.py:50
  31.0 27.1 %collective-permute-start.7 = (bf16[4096,128]{1,0:T(8,128)(2,1)}, bf16[4096,128]{1,0:T(8,128)(2,1)}, u32[]{:S(2)}, u32[]{:S(2)}) collective-permute-start(bf16[4096,128]{1,0:T(8,128)(2,1)} %pad_maximum_fusion.1.refs_3_.refs_5_.refs_7_), channel_id=1, source_target_pairs={{0,64},{1,65},{2,66},{3,67},{4,68},{5,69},{6,70},{7,71},{8,72},{9,... | collective-permute-start | bytes 3145736 | tf_op jit(solution)/shard_map/ppermute | solution.py:50
  32.5 25.7 %collective-permute-start.8 = (bf16[4096,128]{1,0:T(8,128)(2,1)}, bf16[4096,128]{1,0:T(8,128)(2,1)}, u32[]{:S(2)}, u32[]{:S(2)}) collective-permute-start(bf16[4096,128]{1,0:T(8,128)(2,1)} %pad_maximum_fusion.refs_2_.refs_4_.refs_6_), channel_id=1, source_target_pairs={{0,192},{1,193},{2,194},{3,195},{4,196},{5,197},{6,198},{7,199},{8... | collective-permute-start | bytes 3145736 | tf_op jit(solution)/shard_map/ppermute | solution.py:50
  34.7 26.4 %collective-permute-start.9 = (bf16[256,2048]{1,0:T(8,128)(2,1)}, bf16[256,2048]{1,0:T(8,128)(2,1)}, u32[]{:S(2)}, u32[]{:S(2)}) collective-permute-start(bf16[256,2048]{1,0:T(8,128)(2,1)} %get-tuple-element.31), channel_id=1, source_target_pairs={{0,32},{1,33},{2,34},{3,35},{4,36},{5,37},{6,38},{7,39},{8,40},{9,... | collective-permute-start | bytes 3145736 | tf_op jit(solution)/shard_map/ppermute | solution.py:50
  46.6 31.8 %all-to-all-start.1 = ((f16[8,160,256]{2,1,0:T(8,128)(2,1)}), f16[8,160,256]{2,1,0:T(8,128)(2,1)}, u32[]{:S(2)}, u32[]{:S(2)}) async-start(f16[8,160,256]{2,1,0:T(8,128)(2,1)} %multiply_convert_fusion.1), calls=%async_computation.1 | async-start | bytes 1310720 | tf_op jit(solution)/shard_map/all_to_all | solution.py:54
  61.1 6.4 %collective-permute-start.10 = (bf16[256,2048]{1,0:T(8,128)(2,1)}, bf16[256,2048]{1,0:T(8,128)(2,1)S(1)}, u32[]{:S(2)}, u32[]{:S(2)}) collective-permute-start(bf16[256,2048]{1,0:T(8,128)(2,1)} %collective-permute-done.9.refs_4_), channel_id=1, source_target_pairs={{0,1},{1,0},{2,3},{3,2},{4,5},{5,4},{6,7},{7,6},{8,9},{9,8},{10,11... | collective-permute-start | bytes 3145736 | tf_op jit(solution)/shard_map/ppermute | solution.py:50
  61.1 28.5 %collective-permute-start.11 = (bf16[4096,128]{1,0:T(8,128)(2,1)}, bf16[4096,128]{1,0:T(8,128)(2,1)}, u32[]{:S(2)}, u32[]{:S(2)}) collective-permute-start(bf16[4096,128]{1,0:T(8,128)(2,1)} %collective-permute-done.5.refs_6_.refs_8_.refs_4_), channel_id=1, source_target_pairs={{0,64},{1,65},{2,66},{3,67},{4,68},{5,69},{6,70},{7,71},{8,72},{9,... | collective-permute-start | bytes 3145736 | tf_op jit(solution)/shard_map/ppermute | solution.py:50
  61.4 28.2 %collective-permute-start.12 = (bf16[4096,128]{1,0:T(8,128)(2,1)}, bf16[4096,128]{1,0:T(8,128)(2,1)}, u32[]{:S(2)}, u32[]{:S(2)}) collective-permute-start(bf16[4096,128]{1,0:T(8,128)(2,1)} %collective-permute-done.6.refs_7_.refs_9_.refs_5_), channel_id=1, source_target_pairs={{0,192},{1,193},{2,194},{3,195},{4,196},{5,197},{6,198},{7,199},{8... | collective-permute-start | bytes 3145736 | tf_op jit(solution)/shard_map/ppermute | solution.py:50
  64.3 26.8 %collective-permute-start.13 = (bf16[256,2048]{1,0:T(8,128)(2,1)}, bf16[256,2048]{1,0:T(8,128)(2,1)}, u32[]{:S(2)}, u32[]{:S(2)}) collective-permute-start(bf16[256,2048]{1,0:T(8,128)(2,1)} %get-tuple-element.39), channel_id=1, source_target_pairs={{0,32},{1,33},{2,34},{3,35},{4,36},{5,37},{6,38},{7,39},{8,40},{9,... | collective-permute-start | bytes 3145736 | tf_op jit(solution)/shard_map/ppermute | solution.py:50
  81.0 33.0 %all-to-all-start.2 = ((f16[8,224,256]{2,1,0:T(8,128)(2,1)}), f16[8,224,256]{2,1,0:T(8,128)(2,1)}, u32[]{:S(2)}, u32[]{:S(2)}) async-start(f16[8,224,256]{2,1,0:T(8,128)(2,1)} %multiply_convert_fusion), calls=%async_computation.2 | async-start | bytes 1835008 | tf_op jit(solution)/shard_map/all_to_all | solution.py:54
  91.2 11.6 %collective-permute-start.14 = (bf16[256,2048]{1,0:T(8,128)(2,1)}, bf16[256,2048]{1,0:T(8,128)(2,1)}, u32[]{:S(2)}, u32[]{:S(2)}) collective-permute-start(bf16[256,2048]{1,0:T(8,128)(2,1)} %collective-permute-done.13.refs_0_), channel_id=1, source_target_pairs={{0,1},{1,0},{2,3},{3,2},{4,5},{5,4},{6,7},{7,6},{8,9},{9,8},{10,11... | collective-permute-start | bytes 3145736 | tf_op jit(solution)/shard_map/ppermute | solution.py:50
  99.8 10.2 %collective-permute-start.15 = (f16[8,160,128]{2,1,0:T(8,128)(2,1)S(1)}, f16[8,160,128]{2,1,0:T(8,128)(2,1)S(1)}, u32[]{:S(2)}, u32[]{:S(2)}) collective-permute-start(f16[8,160,128]{2,1,0:T(8,128)(2,1)S(1)} %multiply_convert_fusion.4), channel_id=1, source_target_pairs={{0,2},{1,3},{2,0},{3,1},{4,6},{5,7},{6,4},{7,5},{8,10},{9,11},{10,... | collective-permute-start | bytes 983048 | tf_op jit(solution)/shard_map/ppermute | solution.py:50
  114.0 6.4 %collective-permute-start.17 = (f16[8,128,128]{2,1,0:T(8,128)(2,1)S(1)}, f16[8,128,128]{2,1,0:T(8,128)(2,1)S(1)}, u32[]{:S(2)}, u32[]{:S(2)}) collective-permute-start(f16[8,128,128]{2,1,0:T(8,128)(2,1)S(1)} %multiply_convert_fusion.6), channel_id=1, source_target_pairs={{0,2},{1,3},{2,0},{3,1},{4,6},{5,7},{6,4},{7,5},{8,10},{9,11},{10,... | collective-permute-start | bytes 786440 | tf_op jit(solution)/shard_map/ppermute | solution.py:50
  121.4 23.8 %all-to-all-start.3 = ((f16[8,288,128]{2,1,0:T(8,128)(2,1)}), f16[8,288,128]{2,1,0:T(8,128)(2,1)S(1)}, u32[]{:S(2)}, u32[]{:S(2)}) async-start(f16[8,288,128]{2,1,0:T(8,128)(2,1)} %pad_maximum_fusion.2), calls=%async_computation.3 | async-start | bytes 1179648 | tf_op jit(solution)/shard_map/all_to_all | solution.py:54
  128.2 6.8 %collective-permute-start.16 = (f32[480,128]{1,0:T(8,128)S(1)}, f32[480,128]{1,0:T(8,128)S(1)}, u32[]{:S(2)}, u32[]{:S(2)}) collective-permute-start(f32[480,128]{1,0:T(8,128)S(1)} %constant_dynamic-slice_fusion), channel_id=1, source_target_pairs={{0,2},{1,3},{2,0},{3,1},{4,6},{5,7},{6,4},{7,5},{8,10},{9,11},{10,... | collective-permute-start | bytes 737288 | tf_op jit(solution)/shard_map/ppermute | solution.py:50
  135.2 12.9 %collective-permute-start.18 = (f32[192,128]{1,0:T(8,128)S(1)}, f32[192,128]{1,0:T(8,128)S(1)}, u32[]{:S(2)}, u32[]{:S(2)}) collective-permute-start(f32[192,128]{1,0:T(8,128)S(1)} %slice.48), channel_id=1, source_target_pairs={{0,32},{1,33},{2,34},{3,35},{4,36},{5,37},{6,38},{7,39},{8,40},{9,... | collective-permute-start | bytes 294920 | tf_op jit(solution)/shard_map/ppermute | solution.py:50
  145.4 6.2 %collective-permute-start.19 = (f32[192,128]{1,0:T(8,128)S(1)}, f32[192,128]{1,0:T(8,128)S(1)}, u32[]{:S(2)}, u32[]{:S(2)}) collective-permute-start(f32[192,128]{1,0:T(8,128)S(1)} %slice.49), channel_id=1, source_target_pairs={{0,32},{1,33},{2,34},{3,35},{4,36},{5,37},{6,38},{7,39},{8,40},{9,... | collective-permute-start | bytes 294920 | tf_op jit(solution)/shard_map/ppermute | solution.py:50
  154.2 16.3 %all-to-all-start.4 = ((f32[8,96,128]{2,1,0:T(8,128)}), f32[8,96,128]{2,1,0:T(8,128)S(1)}, u32[]{:S(2)}, u32[]{:S(2)}) async-start(f32[8,96,128]{2,1,0:T(8,128)} %shard_map.87), calls=%async_computation.4 | async-start | bytes 786432 | tf_op jit(solution)/shard_map/all_to_all | solution.py:54
  (19 other events, 210.6 us)

commit v5 on v4

--- a/solution.py
+++ b/solution.py
@@ -169,8 +169,8 @@
     ay0, a1, b0, b1, in0 = barrier((ay0, a1, b[0], b[1], in0))
     p2, m2, ay1 = send(b1, X_UP), send(b0, X_DOWN), send(a1, Y_FAR)
     rows, cols = rows + [(ay0, send(ay0, CORE))], cols + [(p1, m1)]
-    new, s0 = barrier((products(rows, cols, PLAN[1]), s0))
-    in1 = half_precision(new, SCALE_CHIP)
+    in1 = half_precision(products(rows, cols, PLAN[1]), SCALE_CHIP)
+    in1, s0 = barrier((in1, s0))
     got1 = over_z(in1)
     p2, m2, ay1, a2, p1, m1, in1 = barrier((p2, m2, ay1, a2, p1, m1, in1))
     p3, m3, ay2 = send(p1, X_UP), send(m1, X_DOWN), send(a2, Y_FAR)

time: 172 us -> 172 us (level)
  no operation moved by 1% of the time
where the time goes in v5:
time: 172 us; the launch traced here: 171 us
  starting transfers between devices  63.1 us (37%)
  waiting for transfers between devices  50.3 us (29%)
  Pallas kernels  34 us (20%)
  other arithmetic  12.5 us (7%)
  local copies, waits for them, and re-layouts  11.1 us (6%)
    all_to_all x5, starting transfers between devices, over_z(): lax.all_to_all(pieces, AXES, 0, 0, axis_index_groups=Z_GROUPS, tiled=True)  35.8 us
    pallas_call x5, Pallas kernels, products(): pl.pallas_call(kernel, out_shape=jax.ShapeDtypeStruct((NZ, 32 * len(plan)...  32.1 us
    ppermute x20, starting transfers between devices, send(): return lax.ppermute(block, AXES, route)  27.3 us
    ppermute x20, waiting for transfers between devices, send(): return lax.ppermute(block, AXES, route)  26.6 us
    all_to_all x5, waiting for transfers between devices, over_z(): lax.all_to_all(pieces, AXES, 0, 0, axis_index_groups=Z_GROUPS, tiled=True)  23.8 us
    unnamed x40, local copies, waits for them, and re-layouts  5.97 us
    convert_element_type x7, other arithmetic, half_precision(): return (block * scale).astype(jnp.float16)  4.83 us
  transfers between devices with their start and end apart: 25, of which 14 were waited for; matrix products, arithmetic and copies ran while one was open for 9% of the time, Pallas kernels for 19%

profile of v5, /device:TPU:32, one launch (start us, length us, event | category | flops | bytes accessed | tf_op | source)
XLA Modules:
  0.0 171.4 jit_solution(2453254827902767507)
XLA Ops:
  3.6 3.2 %collective-permute-start.1 = (bf16[256,2048]{1,0:T(8,128)(2,1)}, bf16[256,2048]{1,0:T(8,128)(2,1)}, u32[]{:S(2)}, u32[]{:S(2)}) collective-permute-start(bf16[256,2048]{1,0:T(8,128)(2,1)} %slice.33), channel_id=1, source_target_pairs={{0,32},{1,33},{2,34},{3,35},{4,36},{5,37},{6,38},{7,39},{8,40},{9,... | collective-permute-start | bytes 3145736 | tf_op jit(solution)/shard_map/ppermute | solution.py:50
  12.2 4.3 %shard_map.82 = f32[8,96,256]{2,1,0:T(8,128)S(1)} custom-call(bf16[768,2048]{1,0:T(8,128)(2,1)S(1)} %copy-done, bf16[768,2048]{1,0:T(8,128)(2,1)} %collective-permute-done.refs_1_, bf16[4096,128]{1,0:T(8,128)(2,1)} %pad_maximum_fusion.refs_2_.refs_4_.refs_6_, bf16[4096,128]{1,0:T(8,128)(2,1)} %pad_maximum_fusion.1.refs_3_.refs_5_.refs_7_), custom_call_target="tpu_custom_call" | custom-call | flops 1 | bytes 1 | tf_op jit(solution)/shard_map/pallas_call | solution.py:83
  17.3 8.6 %all-to-all-start = ((f16[8,96,256]{2,1,0:T(8,128)(2,1)}), f16[8,96,256]{2,1,0:T(8,128)(2,1)S(1)}, u32[]{:S(2)}, u32[]{:S(2)}) async-start(f16[8,96,256]{2,1,0:T(8,128)(2,1)} %multiply_convert_fusion.2), calls=%async_computation | async-start | bytes 786432 | tf_op jit(solution)/shard_map/all_to_all | solution.py:54
  27.4 3.7 %collective-permute-done.1.refs_2_ = bf16[256,2048]{1,0:T(8,128)(2,1)} collective-permute-done((bf16[256,2048]{1,0:T(8,128)(2,1)}, bf16[256,2048]{1,0:T(8,128)(2,1)}, u32[]{:S(2)}, u32[]{:S(2)}) %collective-permute-start.1) | collective-permute-done | bytes 1048608 | tf_op jit(solution)/shard_map/ppermute | solution.py:50
  34.7 2.7 %collective-permute-start.9 = (bf16[256,2048]{1,0:T(8,128)(2,1)}, bf16[256,2048]{1,0:T(8,128)(2,1)}, u32[]{:S(2)}, u32[]{:S(2)}) collective-permute-start(bf16[256,2048]{1,0:T(8,128)(2,1)} %get-tuple-element.31), channel_id=1, source_target_pairs={{0,32},{1,33},{2,34},{3,35},{4,36},{5,37},{6,38},{7,39},{8,40},{9,... | collective-permute-start | bytes 3145736 | tf_op jit(solution)/shard_map/ppermute | solution.py:50
  39.0 6.5 %shard_map.83 = f32[8,160,256]{2,1,0:T(8,128)S(1)} custom-call(bf16[768,2048]{1,0:T(8,128)(2,1)S(1)} %copy-done, bf16[768,2048]{1,0:T(8,128)(2,1)} %collective-permute-done.refs_1_, bf16[256,2048]{1,0:T(8,128)(2,1)} %collective-permute-done.1.refs_2_, bf16[256,2048]{1,0:T(8,128)(2,1)} %collective-permute-done.4.refs_3_, ...), custom_call_target="tpu_custom_call" | custom-call | flops 1 | bytes 1 | tf_op jit(solution)/shard_map/pallas_call | solution.py:83
  46.6 7.1 %all-to-all-start.1 = ((f16[8,160,256]{2,1,0:T(8,128)(2,1)}), f16[8,160,256]{2,1,0:T(8,128)(2,1)}, u32[]{:S(2)}, u32[]{:S(2)}) async-start(f16[8,160,256]{2,1,0:T(8,128)(2,1)} %multiply_convert_fusion.1), calls=%async_computation.1 | async-start | bytes 1310720 | tf_op jit(solution)/shard_map/all_to_all | solution.py:54
  53.7 4.4 %collective-permute-done.7.refs_11_.refs_7_ = bf16[4096,128]{1,0:T(8,128)(2,1)} collective-permute-done((bf16[4096,128]{1,0:T(8,128)(2,1)}, bf16[4096,128]{1,0:T(8,128)(2,1)}, u32[]{:S(2)}, u32[]{:S(2)}) %collective-permute-start.7) | collective-permute-done | bytes 1048608 | tf_op jit(solution)/shard_map/ppermute | solution.py:50
  58.3 2.8 %collective-permute-done.9.refs_4_ = bf16[256,2048]{1,0:T(8,128)(2,1)} collective-permute-done((bf16[256,2048]{1,0:T(8,128)(2,1)}, bf16[256,2048]{1,0:T(8,128)(2,1)}, u32[]{:S(2)}, u32[]{:S(2)}) %collective-permute-start.9) | collective-permute-done | bytes 1048608 | tf_op jit(solution)/shard_map/ppermute | solution.py:50
  61.4 3.0 %collective-permute-start.12 = (bf16[4096,128]{1,0:T(8,128)(2,1)}, bf16[4096,128]{1,0:T(8,128)(2,1)}, u32[]{:S(2)}, u32[]{:S(2)}) collective-permute-start(bf16[4096,128]{1,0:T(8,128)(2,1)} %collective-permute-done.6.refs_7_.refs_9_.refs_5_), channel_id=1, source_target_pairs={{0,192},{1,193},{2,194},{3,195},{4,196},{5,197},{6,198},{7,199},{8... | collective-permute-start | bytes 3145736 | tf_op jit(solution)/shard_map/ppermute | solution.py:50
  64.3 3.2 %collective-permute-start.13 = (bf16[256,2048]{1,0:T(8,128)(2,1)}, bf16[256,2048]{1,0:T(8,128)(2,1)}, u32[]{:S(2)}, u32[]{:S(2)}) collective-permute-start(bf16[256,2048]{1,0:T(8,128)(2,1)} %get-tuple-element.39), channel_id=1, source_target_pairs={{0,32},{1,33},{2,34},{3,35},{4,36},{5,37},{6,38},{7,39},{8,40},{9,... | collective-permute-start | bytes 3145736 | tf_op jit(solution)/shard_map/ppermute | solution.py:50
  67.5 8.5 %shard_map.84 = f32[8,224,256]{2,1,0:T(8,128)S(1)} custom-call(bf16[768,2048]{1,0:T(8,128)(2,1)S(1)} %copy-done, bf16[768,2048]{1,0:T(8,128)(2,1)} %collective-permute-done.refs_1_, bf16[256,2048]{1,0:T(8,128)(2,1)} %collective-permute-done.1.refs_2_, bf16[256,2048]{1,0:T(8,128)(2,1)} %collective-permute-done.4.refs_3_, ...), custom_call_target="tpu_custom_call" | custom-call | flops 1 | bytes 1 | tf_op jit(solution)/shard_map/pallas_call | solution.py:83
  78.3 2.6 %multiply_convert_fusion = f16[8,224,256]{2,1,0:T(8,128)(2,1)} fusion(f32[8,224,256]{2,1,0:T(8,128)} %copy-done.1), kind=kLoop, calls=%fused_computation.1 | loop fusion | flops 917504 | bytes 2752512 | tf_op jit(solution)/shard_map/convert_element_type | solution.py:94
  81.0 8.6 %all-to-all-start.2 = ((f16[8,224,256]{2,1,0:T(8,128)(2,1)}), f16[8,224,256]{2,1,0:T(8,128)(2,1)}, u32[]{:S(2)}, u32[]{:S(2)}) async-start(f16[8,224,256]{2,1,0:T(8,128)(2,1)} %multiply_convert_fusion), calls=%async_computation.2 | async-start | bytes 1835008 | tf_op jit(solution)/shard_map/all_to_all | solution.py:54
  92.4 6.3 %shard_map.86 = f32[8,160,256]{2,1,0:T(8,128)S(1)} custom-call(bf16[768,2048]{1,0:T(8,128)(2,1)S(1)} %copy-done, bf16[768,2048]{1,0:T(8,128)(2,1)} %collective-permute-done.refs_1_, bf16[256,2048]{1,0:T(8,128)(2,1)} %collective-permute-done.1.refs_2_, bf16[256,2048]{1,0:T(8,128)(2,1)} %collective-permute-done.4.refs_3_, ...), custom_call_target="tpu_custom_call" | custom-call | flops 1 | bytes 1 | tf_op jit(solution)/shard_map/pallas_call | solution.py:83
  102.7 6.5 %shard_map.85 = f32[8,128,256]{2,1,0:T(8,128)S(1)} custom-call(bf16[256,2048]{1,0:T(8,128)(2,1)} %collective-permute-done.13.refs_0_, bf16[256,2048]{1,0:T(8,128)(2,1)} %collective-permute-done.14.refs_1_, bf16[4096,128]{1,0:T(8,128)(2,1)} %pad_maximum_fusion.refs_2_.refs_4_.refs_6_, bf16[4096,128]{1,0:T(8,128)(2,1)} %pad_maximum_fusion.1.refs_3_.refs_5_.refs_7_, ...), custom_call_target="tpu_custom_call" | custom-call | flops 1 | bytes 1 | tf_op jit(solution)/shard_map/pallas_call | solution.py:83
  110.0 3.9 %all-to-all-done.2 = f16[8,224,256]{2,1,0:T(8,128)(2,1)} async-done(((f16[8,224,256]{2,1,0:T(8,128)(2,1)}), f16[8,224,256]{2,1,0:T(8,128)(2,1)}, u32[]{:S(2)}, u32[]{:S(2)}) %all-to-all-start.2) | async-done | bytes 917536 | tf_op jit(solution)/shard_map/all_to_all | solution.py:54
  116.8 3.5 %collective-permute-done.17 = f16[8,128,128]{2,1,0:T(8,128)(2,1)S(1)} collective-permute-done((f16[8,128,128]{2,1,0:T(8,128)(2,1)S(1)}, f16[8,128,128]{2,1,0:T(8,128)(2,1)S(1)}, u32[]{:S(2)}, u32[]{:S(2)}) %collective-permute-start.17) | collective-permute-done | bytes 262176 | tf_op jit(solution)/shard_map/ppermute | solution.py:50
  121.4 6.8 %all-to-all-start.3 = ((f16[8,288,128]{2,1,0:T(8,128)(2,1)}), f16[8,288,128]{2,1,0:T(8,128)(2,1)S(1)}, u32[]{:S(2)}, u32[]{:S(2)}) async-start(f16[8,288,128]{2,1,0:T(8,128)(2,1)} %pad_maximum_fusion.2), calls=%async_computation.3 | async-start | bytes 1179648 | tf_op jit(solution)/shard_map/all_to_all | solution.py:54
  129.4 5.7 %collective-permute-done.16 = f32[480,128]{1,0:T(8,128)S(1)} collective-permute-done((f32[480,128]{1,0:T(8,128)S(1)}, f32[480,128]{1,0:T(8,128)S(1)}, u32[]{:S(2)}, u32[]{:S(2)}) %collective-permute-start.16) | collective-permute-done | bytes 245792 | tf_op jit(solution)/shard_map/ppermute | solution.py:50
  137.4 7.9 %all-to-all-done.3 = f16[8,288,128]{2,1,0:T(8,128)(2,1)S(1)} async-done(((f16[8,288,128]{2,1,0:T(8,128)(2,1)}), f16[8,288,128]{2,1,0:T(8,128)(2,1)S(1)}, u32[]{:S(2)}, u32[]{:S(2)}) %all-to-all-start.3) | async-done | bytes 589856 | tf_op jit(solution)/shard_map/all_to_all | solution.py:54
  148.1 3.5 %collective-permute-done.19.late_far_ref = f32[192,128]{1,0:T(8,128)S(1)} collective-permute-done((f32[192,128]{1,0:T(8,128)S(1)}, f32[192,128]{1,0:T(8,128)S(1)}, u32[]{:S(2)}, u32[]{:S(2)}) %collective-permute-start.19) | collective-permute-done | bytes 98336 | tf_op jit(solution)/shard_map/ppermute | solution.py:50
  154.2 4.8 %all-to-all-start.4 = ((f32[8,96,128]{2,1,0:T(8,128)}), f32[8,96,128]{2,1,0:T(8,128)S(1)}, u32[]{:S(2)}, u32[]{:S(2)}) async-start(f32[8,96,128]{2,1,0:T(8,128)} %shard_map.87), calls=%async_computation.4 | async-start | bytes 786432 | tf_op jit(solution)/shard_map/all_to_all | solution.py:54
  160.0 10.5 %all-to-all-done.4 = f32[8,96,128]{2,1,0:T(8,128)S(1)} async-done(((f32[8,96,128]{2,1,0:T(8,128)}), f32[8,96,128]{2,1,0:T(8,128)S(1)}, u32[]{:S(2)}, u32[]{:S(2)}) %all-to-all-start.4) | async-done | bytes 393248 | tf_op jit(solution)/shard_map/all_to_all | solution.py:54
  (113 shorter events, 42.5 us)
Async XLA Ops:
  0.0 12.2 %collective-permute-start = (bf16[768,2048]{1,0:T(8,128)(2,1)}, bf16[768,2048]{1,0:T(8,128)(2,1)}, u32[]{:S(2)}, u32[]{:S(2)}) collective-permute-start(bf16[768,2048]{1,0:T(8,128)(2,1)} %refs_0_.7), channel_id=1, source_target_pairs={{0,1},{1,0},{2,3},{3,2},{4,5},{5,4},{6,7},{7,6},{8,9},{9,8},{10,11... | collective-permute-start | bytes 9437192 | tf_op jit(solution)/shard_map/ppermute | solution.py:50
  2.5 6.9 %collective-permute-start.3 = (bf16[2048,128]{1,0:T(8,128)(2,1)S(1)}, bf16[2048,128]{1,0:T(8,128)(2,1)S(1)}, u32[]{:S(2)}, u32[]{:S(2)}) collective-permute-start(bf16[2048,128]{1,0:T(8,128)(2,1)S(1)} %get-tuple-element.58), channel_id=1, source_target_pairs={{0,1},{1,0},{2,3},{3,2},{4,5},{5,4},{6,7},{7,6},{8,9},{9,8},{10,11... | collective-permute-start | bytes 1572872 | tf_op jit(solution)/shard_map/ppermute | solution.py:50
  3.6 27.4 %collective-permute-start.1 = (bf16[256,2048]{1,0:T(8,128)(2,1)}, bf16[256,2048]{1,0:T(8,128)(2,1)}, u32[]{:S(2)}, u32[]{:S(2)}) collective-permute-start(bf16[256,2048]{1,0:T(8,128)(2,1)} %slice.33), channel_id=1, source_target_pairs={{0,32},{1,33},{2,34},{3,35},{4,36},{5,37},{6,38},{7,39},{8,40},{9,... | collective-permute-start | bytes 3145736 | tf_op jit(solution)/shard_map/ppermute | solution.py:50
  7.9 26.8 %collective-permute-start.5 = (bf16[4096,128]{1,0:T(8,128)(2,1)}, bf16[4096,128]{1,0:T(8,128)(2,1)}, u32[]{:S(2)}, u32[]{:S(2)}) collective-permute-start(bf16[4096,128]{1,0:T(8,128)(2,1)} %pad_maximum_fusion.refs_2_.refs_4_.refs_6_), channel_id=1, source_target_pairs={{0,64},{1,65},{2,66},{3,67},{4,68},{5,69},{6,70},{7,71},{8,72},{9,... | collective-permute-start | bytes 3145736 | tf_op jit(solution)/shard_map/ppermute | solution.py:50
  10.5 28.6 %collective-permute-start.6 = (bf16[4096,128]{1,0:T(8,128)(2,1)}, bf16[4096,128]{1,0:T(8,128)(2,1)}, u32[]{:S(2)}, u32[]{:S(2)}) collective-permute-start(bf16[4096,128]{1,0:T(8,128)(2,1)} %pad_maximum_fusion.1.refs_3_.refs_5_.refs_7_), channel_id=1, source_target_pairs={{0,192},{1,193},{2,194},{3,195},{4,196},{5,197},{6,198},{7,199},{8... | collective-permute-start | bytes 3145736 | tf_op jit(solution)/shard_map/ppermute | solution.py:50
  17.3 21.6 %all-to-all-start = ((f16[8,96,256]{2,1,0:T(8,128)(2,1)}), f16[8,96,256]{2,1,0:T(8,128)(2,1)S(1)}, u32[]{:S(2)}, u32[]{:S(2)}) async-start(f16[8,96,256]{2,1,0:T(8,128)(2,1)} %multiply_convert_fusion.2), calls=%async_computation | async-start | bytes 786432 | tf_op jit(solution)/shard_map/all_to_all | solution.py:54
  31.0 8.0 %collective-permute-start.4 = (bf16[256,2048]{1,0:T(8,128)(2,1)}, bf16[256,2048]{1,0:T(8,128)(2,1)}, u32[]{:S(2)}, u32[]{:S(2)}) collective-permute-start(bf16[256,2048]{1,0:T(8,128)(2,1)} %collective-permute-done.1.refs_2_), channel_id=1, source_target_pairs={{0,1},{1,0},{2,3},{3,2},{4,5},{5,4},{6,7},{7,6},{8,9},{9,8},{10,11... | collective-permute-start | bytes 3145736 | tf_op jit(solution)/shard_map/ppermute | solution.py:50
  31.0 27.1 %collective-permute-start.7 = (bf16[4096,128]{1,0:T(8,128)(2,1)}, bf16[4096,128]{1,0:T(8,128)(2,1)}, u32[]{:S(2)}, u32[]{:S(2)}) collective-permute-start(bf16[4096,128]{1,0:T(8,128)(2,1)} %pad_maximum_fusion.1.refs_3_.refs_5_.refs_7_), channel_id=1, source_target_pairs={{0,64},{1,65},{2,66},{3,67},{4,68},{5,69},{6,70},{7,71},{8,72},{9,... | collective-permute-start | bytes 3145736 | tf_op jit(solution)/shard_map/ppermute | solution.py:50
  32.5 25.7 %collective-permute-start.8 = (bf16[4096,128]{1,0:T(8,128)(2,1)}, bf16[4096,128]{1,0:T(8,128)(2,1)}, u32[]{:S(2)}, u32[]{:S(2)}) collective-permute-start(bf16[4096,128]{1,0:T(8,128)(2,1)} %pad_maximum_fusion.refs_2_.refs_4_.refs_6_), channel_id=1, source_target_pairs={{0,192},{1,193},{2,194},{3,195},{4,196},{5,197},{6,198},{7,199},{8... | collective-permute-start | bytes 3145736 | tf_op jit(solution)/shard_map/ppermute | solution.py:50
  34.7 26.4 %collective-permute-start.9 = (bf16[256,2048]{1,0:T(8,128)(2,1)}, bf16[256,2048]{1,0:T(8,128)(2,1)}, u32[]{:S(2)}, u32[]{:S(2)}) collective-permute-start(bf16[256,2048]{1,0:T(8,128)(2,1)} %get-tuple-element.31), channel_id=1, source_target_pairs={{0,32},{1,33},{2,34},{3,35},{4,36},{5,37},{6,38},{7,39},{8,40},{9,... | collective-permute-start | bytes 3145736 | tf_op jit(solution)/shard_map/ppermute | solution.py:50
  46.6 31.8 %all-to-all-start.1 = ((f16[8,160,256]{2,1,0:T(8,128)(2,1)}), f16[8,160,256]{2,1,0:T(8,128)(2,1)}, u32[]{:S(2)}, u32[]{:S(2)}) async-start(f16[8,160,256]{2,1,0:T(8,128)(2,1)} %multiply_convert_fusion.1), calls=%async_computation.1 | async-start | bytes 1310720 | tf_op jit(solution)/shard_map/all_to_all | solution.py:54
  61.1 6.4 %collective-permute-start.10 = (bf16[256,2048]{1,0:T(8,128)(2,1)}, bf16[256,2048]{1,0:T(8,128)(2,1)S(1)}, u32[]{:S(2)}, u32[]{:S(2)}) collective-permute-start(bf16[256,2048]{1,0:T(8,128)(2,1)} %collective-permute-done.9.refs_4_), channel_id=1, source_target_pairs={{0,1},{1,0},{2,3},{3,2},{4,5},{5,4},{6,7},{7,6},{8,9},{9,8},{10,11... | collective-permute-start | bytes 3145736 | tf_op jit(solution)/shard_map/ppermute | solution.py:50
  61.1 28.5 %collective-permute-start.11 = (bf16[4096,128]{1,0:T(8,128)(2,1)}, bf16[4096,128]{1,0:T(8,128)(2,1)}, u32[]{:S(2)}, u32[]{:S(2)}) collective-permute-start(bf16[4096,128]{1,0:T(8,128)(2,1)} %collective-permute-done.5.refs_6_.refs_8_.refs_4_), channel_id=1, source_target_pairs={{0,64},{1,65},{2,66},{3,67},{4,68},{5,69},{6,70},{7,71},{8,72},{9,... | collective-permute-start | bytes 3145736 | tf_op jit(solution)/shard_map/ppermute | solution.py:50
  61.4 28.2 %collective-permute-start.12 = (bf16[4096,128]{1,0:T(8,128)(2,1)}, bf16[4096,128]{1,0:T(8,128)(2,1)}, u32[]{:S(2)}, u32[]{:S(2)}) collective-permute-start(bf16[4096,128]{1,0:T(8,128)(2,1)} %collective-permute-done.6.refs_7_.refs_9_.refs_5_), channel_id=1, source_target_pairs={{0,192},{1,193},{2,194},{3,195},{4,196},{5,197},{6,198},{7,199},{8... | collective-permute-start | bytes 3145736 | tf_op jit(solution)/shard_map/ppermute | solution.py:50
  64.3 26.8 %collective-permute-start.13 = (bf16[256,2048]{1,0:T(8,128)(2,1)}, bf16[256,2048]{1,0:T(8,128)(2,1)}, u32[]{:S(2)}, u32[]{:S(2)}) collective-permute-start(bf16[256,2048]{1,0:T(8,128)(2,1)} %get-tuple-element.39), channel_id=1, source_target_pairs={{0,32},{1,33},{2,34},{3,35},{4,36},{5,37},{6,38},{7,39},{8,40},{9,... | collective-permute-start | bytes 3145736 | tf_op jit(solution)/shard_map/ppermute | solution.py:50
  81.0 33.0 %all-to-all-start.2 = ((f16[8,224,256]{2,1,0:T(8,128)(2,1)}), f16[8,224,256]{2,1,0:T(8,128)(2,1)}, u32[]{:S(2)}, u32[]{:S(2)}) async-start(f16[8,224,256]{2,1,0:T(8,128)(2,1)} %multiply_convert_fusion), calls=%async_computation.2 | async-start | bytes 1835008 | tf_op jit(solution)/shard_map/all_to_all | solution.py:54
  91.2 11.6 %collective-permute-start.14 = (bf16[256,2048]{1,0:T(8,128)(2,1)}, bf16[256,2048]{1,0:T(8,128)(2,1)}, u32[]{:S(2)}, u32[]{:S(2)}) collective-permute-start(bf16[256,2048]{1,0:T(8,128)(2,1)} %collective-permute-done.13.refs_0_), channel_id=1, source_target_pairs={{0,1},{1,0},{2,3},{3,2},{4,5},{5,4},{6,7},{7,6},{8,9},{9,8},{10,11... | collective-permute-start | bytes 3145736 | tf_op jit(solution)/shard_map/ppermute | solution.py:50
  99.8 10.2 %collective-permute-start.15 = (f16[8,160,128]{2,1,0:T(8,128)(2,1)S(1)}, f16[8,160,128]{2,1,0:T(8,128)(2,1)S(1)}, u32[]{:S(2)}, u32[]{:S(2)}) collective-permute-start(f16[8,160,128]{2,1,0:T(8,128)(2,1)S(1)} %multiply_convert_fusion.4), channel_id=1, source_target_pairs={{0,2},{1,3},{2,0},{3,1},{4,6},{5,7},{6,4},{7,5},{8,10},{9,11},{10,... | collective-permute-start | bytes 983048 | tf_op jit(solution)/shard_map/ppermute | solution.py:50
  114.0 6.4 %collective-permute-start.17 = (f16[8,128,128]{2,1,0:T(8,128)(2,1)S(1)}, f16[8,128,128]{2,1,0:T(8,128)(2,1)S(1)}, u32[]{:S(2)}, u32[]{:S(2)}) collective-permute-start(f16[8,128,128]{2,1,0:T(8,128)(2,1)S(1)} %multiply_convert_fusion.6), channel_id=1, source_target_pairs={{0,2},{1,3},{2,0},{3,1},{4,6},{5,7},{6,4},{7,5},{8,10},{9,11},{10,... | collective-permute-start | bytes 786440 | tf_op jit(solution)/shard_map/ppermute | solution.py:50
  121.4 23.8 %all-to-all-start.3 = ((f16[8,288,128]{2,1,0:T(8,128)(2,1)}), f16[8,288,128]{2,1,0:T(8,128)(2,1)S(1)}, u32[]{:S(2)}, u32[]{:S(2)}) async-start(f16[8,288,128]{2,1,0:T(8,128)(2,1)} %pad_maximum_fusion.2), calls=%async_computation.3 | async-start | bytes 1179648 | tf_op jit(solution)/shard_map/all_to_all | solution.py:54
  128.2 6.8 %collective-permute-start.16 = (f32[480,128]{1,0:T(8,128)S(1)}, f32[480,128]{1,0:T(8,128)S(1)}, u32[]{:S(2)}, u32[]{:S(2)}) collective-permute-start(f32[480,128]{1,0:T(8,128)S(1)} %constant_dynamic-slice_fusion), channel_id=1, source_target_pairs={{0,2},{1,3},{2,0},{3,1},{4,6},{5,7},{6,4},{7,5},{8,10},{9,11},{10,... | collective-permute-start | bytes 737288 | tf_op jit(solution)/shard_map/ppermute | solution.py:50
  135.2 12.9 %collective-permute-start.18 = (f32[192,128]{1,0:T(8,128)S(1)}, f32[192,128]{1,0:T(8,128)S(1)}, u32[]{:S(2)}, u32[]{:S(2)}) collective-permute-start(f32[192,128]{1,0:T(8,128)S(1)} %slice.48), channel_id=1, source_target_pairs={{0,32},{1,33},{2,34},{3,35},{4,36},{5,37},{6,38},{7,39},{8,40},{9,... | collective-permute-start | bytes 294920 | tf_op jit(solution)/shard_map/ppermute | solution.py:50
  145.4 6.2 %collective-permute-start.19 = (f32[192,128]{1,0:T(8,128)S(1)}, f32[192,128]{1,0:T(8,128)S(1)}, u32[]{:S(2)}, u32[]{:S(2)}) collective-permute-start(f32[192,128]{1,0:T(8,128)S(1)} %slice.49), channel_id=1, source_target_pairs={{0,32},{1,33},{2,34},{3,35},{4,36},{5,37},{6,38},{7,39},{8,40},{9,... | collective-permute-start | bytes 294920 | tf_op jit(solution)/shard_map/ppermute | solution.py:50
  154.2 16.3 %all-to-all-start.4 = ((f32[8,96,128]{2,1,0:T(8,128)}), f32[8,96,128]{2,1,0:T(8,128)S(1)}, u32[]{:S(2)}, u32[]{:S(2)}) async-start(f32[8,96,128]{2,1,0:T(8,128)} %shard_map.87), calls=%async_computation.4 | async-start | bytes 786432 | tf_op jit(solution)/shard_map/all_to_all | solution.py:54
  (19 other events, 210.6 us)
